TPU v7x, 512 devices: a whole 4x8x8 slice. The times are simulated.
512 devices in a mesh: row: 32 (over y, x), col: 16 (over z, core).
Axes of the slice: x: 4, y: 8, z: 8, core: 2. Of those that a mesh axis runs over, the one named last changes fastest.
Arguments:
- diag_tiles: float32 [32, 256, 256], P('row'), as said below
- left_fac: bfloat16 [32, 32, 256, 128], P('row', 'col'), as said below
- right_fac: bfloat16 [32, 32, 256, 128], P('row', 'col'), as said below
- ranks: int32 [32, 32], replicated, may hold values from 16 to 128, as said below
Outputs:
- factored: float32 [32, 32, 256, 256], P('row', 'col')
Inputs may be any that keep to these rules, and one draw needn't show every extreme that they name: `ranks`: every entry is a multiple of 16; in every draw some tile below the diagonal has rank 128, and the mean rank is about a third of 128. `diag_tiles`: every tile is symmetric; the first diagonal tile and the updated second diagonal tile M are positive definite. `left_fac`: entries have mean zero and deviation one. `right_fac`: entries have mean zero and deviation one over the square root of 128.
All inputs are finite; a program needn't handle non-finite values.
Results may differ from a plain program's by a relative error of at most 0.0003.
Values sent between devices are 32-bit elements; how exact they have to be, the bound alone decides.
A program may use at most 64 MiB of HBM per device.

v0:
```python
import jax
import jax.numpy as jnp
from jax import lax
from jax.sharding import PartitionSpec as P

PRECISE = lax.Precision.HIGHEST


def from_root(shard, axis, root):
    mine = lax.axis_index(axis) == root
    return lax.psum(jnp.where(mine, shard, jnp.zeros_like(shard)), axis)


def lower_solve(factor, stacked):
    pieces, tile_width, rank_cap = stacked.shape
    flattened = jnp.transpose(stacked, (1, 0, 2)).reshape(tile_width, pieces * rank_cap)
    solved = lax.linalg.triangular_solve(factor, flattened, left_side=True, lower=True)
    return jnp.transpose(solved.reshape(tile_width, pieces, rank_cap), (1, 0, 2))


def expand(left_basis, weights):
    return jnp.einsum("nbr,ncr->nbc", left_basis, weights, precision=PRECISE)


def correction(head_basis, row_solved, pivot_solved):
    mixing = jnp.einsum("nbr,bs->nrs", row_solved, pivot_solved, precision=PRECISE)
    return -jnp.einsum("bs,nrs->nbr", head_basis, mixing, precision=PRECISE)


def take_slot(stacked, holder_slot):
    return lax.dynamic_index_in_dim(stacked, holder_slot, 0, keepdims=False)


def shards(diag_tiles, left_fac, right_fac, ranks):
    grid_rows = lax.axis_size("row")
    grid_cols = lax.axis_size("col")
    row_here = lax.axis_index("row")
    col_here = lax.axis_index("col")
    row_slots, col_slots, tile_width, rank_cap = left_fac.shape
    tile_rows = jnp.arange(row_slots, dtype=jnp.int32) * grid_rows + row_here
    tile_cols = jnp.arange(col_slots, dtype=jnp.int32) * grid_cols + col_here
    local_ranks = jnp.take(jnp.take(ranks, tile_rows, axis=0), tile_cols, axis=1)
    columns_live = jnp.arange(rank_cap, dtype=jnp.int32)[None, None, :] < local_ranks[:, :, None]
    left_bases = jnp.where(columns_live[:, :, None, :], left_fac.astype(jnp.float32), 0.0)
    right_coefs = right_fac.astype(jnp.float32)
    first_pivot = from_root(jnp.linalg.cholesky(diag_tiles[0]), "row", 0)
    first_local = lower_solve(first_pivot, right_coefs[:, 0])
    first_row_basis, first_row_solved = (
        from_root(left_bases[:, 0], "col", 0),
        from_root(first_local, "col", 0),
    )
    gathered_basis = []
    gathered_solved = []
    for column_slot in range(col_slots):
        tile_number = column_slot * grid_cols + col_here
        holder_slot = tile_number // grid_rows
        received = (
            from_root(take_slot(first_row_basis, holder_slot), "row", tile_number % grid_rows),
            from_root(take_slot(first_row_solved, holder_slot), "row", tile_number % grid_rows),
        )
        gathered_basis.append(received[0])
        gathered_solved.append(received[1])
    first_col_basis = jnp.stack(gathered_basis)
    first_col_solved = jnp.stack(gathered_solved)
    pivot_basis = first_row_basis[0]
    pivot_solved = first_row_solved[0]
    pivot_cross = jnp.einsum("br,bs->rs", pivot_solved, pivot_solved, precision=PRECISE)
    partial_term = jnp.matmul(pivot_basis, pivot_cross, precision=PRECISE)
    shifted = diag_tiles[0] - jnp.matmul(partial_term, pivot_basis.T, precision=PRECISE)
    second_pivot = from_root(jnp.linalg.cholesky(shifted), "row", 1)
    second_local = lower_solve(second_pivot, right_coefs[:, 0])
    first_row_dense = expand(first_row_basis, first_row_solved)
    first_col_dense = expand(first_col_basis, first_col_solved)
    pieces_dense = []
    local_head = lax.linalg.triangular_solve(
        second_pivot, first_col_basis[0], left_side=True, lower=True
    )
    local_minus = correction(local_head, first_row_solved, first_col_solved[0])
    second_row = (
        from_root(left_bases[:, 0], "col", 1),
        from_root(second_local, "col", 1),
        from_root(local_minus, "col", 1),
    )
    second_row_dense = expand(second_row[0], second_row[1]) + expand(first_row_basis, second_row[2])
    for column_slot in range(col_slots):
        tile_number = column_slot * grid_cols + col_here
        holder_slot = tile_number // grid_rows
        received = (
            from_root(take_slot(second_row[0], holder_slot), "row", tile_number % grid_rows),
            from_root(take_slot(second_row[1], holder_slot), "row", tile_number % grid_rows),
            from_root(take_slot(second_row[2], holder_slot), "row", tile_number % grid_rows),
        )
        own_dense = expand(received[0][None], received[1][None]) + expand(
            first_col_basis[column_slot][None], received[2][None]
        )
        pieces_dense.append(own_dense[0])
    second_col_dense = jnp.stack(pieces_dense)
    dense_front = jnp.einsum("lmbr,lmcr->lmbc", left_bases, right_coefs, precision=PRECISE)
    updates = jnp.einsum("lbk,mck->lmbc", first_row_dense, first_col_dense, precision=PRECISE)
    updates = updates + jnp.einsum(
        "lbk,mck->lmbc", second_row_dense, second_col_dense, precision=PRECISE
    )
    schur = dense_front - updates
    row_ids = tile_rows[:, None, None, None]
    col_ids = tile_cols[None, :, None, None]
    chosen = jnp.where(
        col_ids == 0,
        first_row_dense[:, None],
        jnp.where(col_ids == 1, second_row_dense[:, None], schur),
    )
    return jnp.where(col_ids < row_ids, chosen, 0.0)


def solution(mesh):
    in_specs = (P("row", None, None), P("row", "col", None, None), P("row", "col", None, None), P())
    out_specs = P("row", "col", None, None)
    return jax.shard_map(shards, mesh=mesh, in_specs=in_specs, out_specs=out_specs, check_vma=False)
```

profile of v0, /device:TPU:1, one launch (start us, length us, event | category | flops | bytes accessed | tf_op | source)
XLA Modules:
  0.0 861.9 jit_solution(8564235674343520192)
XLA Ops:
  6.5 1.1 copy.12
  7.8 11.7 %cholesky.130 = f32[128,128]{1,0:T(8,128)S(1)} custom-call(f32[128,128]{1,0:T(8,128)S(1)} %cholesky.194), custom_call_target="Cholesky" | custom-call | tf_op jit(solution)/shard_map/jit(cholesky)/cholesky | solution.py:46
  19.5 9.8 %custom-call.14 = f32[1,128,128]{1,2,0:T(8,128)S(1)} custom-call(f32[1,128,128]{2,1,0:T(8,128)S(1)} %get-tuple-element.96), custom_call_target="InvertDiagBlocksLowerTriangular" | custom-call | tf_op jit(solution)/shard_map/jit(cholesky)/cholesky | solution.py:46
  29.8 11.7 %cholesky.147 = f32[128,128]{1,0:T(8,128)S(1)} custom-call(f32[128,128]{1,0:T(8,128)S(1)} %convolution_subtract_fusion.5), custom_call_target="Cholesky" | custom-call | tf_op jit(solution)/shard_map/jit(cholesky)/cholesky | solution.py:46
  47.6 153.1 %all-reduce.11.cloned.1.call-done = f32[256,256]{1,0:T(8,128)} async-done(((f32[256,256]{1,0:T(8,128)}), f32[256,256]{1,0:T(8,128)}) %all-reduce.11.cloned.1.call-update) | async-done | bytes 262160 | tf_op jit(solution)/shard_map/psum | solution.py:11
  201.8 4.1 while.7
  202.4 1.4 bitcast_dynamic-update-slice_fusion.4
  204.4 1.4 bitcast_dynamic-update-slice_fusion.4
  205.9 19.7 %custom-call.15 = f32[2,128,128]{1,2,0:T(8,128)S(1)} custom-call(f32[2,128,128]{2,1,0:T(8,128)S(1)} %get-tuple-element.38), custom_call_target="InvertDiagBlocksLowerTriangular" | custom-call | tf_op jit(solution)/shard_map/triangular_solve/custom-call.0 | solution.py:17
  227.1 116.7 %all-reduce.19.cloned.1.call-done = (f32[256,128]{1,0:T(8,128)}, f32[256,128]{1,0:T(8,128)}) async-done(((f32[256,128]{1,0:T(8,128)}, f32[256,128]{1,0:T(8,128)}), (f32[256,128]{1,0:T(8,128)}, f32[256,128]{1,0:T(8,128)})) %all-reduce.19.cloned.1.call-update) | async-done | bytes 262160 | tf_op jit(solution)/shard_map/psum | solution.py:11
  343.8 1.4 fusion.60
  347.8 11.7 %cholesky.164 = f32[128,128]{1,0:T(8,128)S(1)} custom-call(f32[128,128]{1,0:T(8,128)S(1)} %cholesky.197), custom_call_target="Cholesky" | custom-call | tf_op jit(solution)/shard_map/jit(cholesky)/cholesky | solution.py:70
  359.6 9.8 %custom-call.16 = f32[1,128,128]{1,2,0:T(8,128)S(1)} custom-call(f32[1,128,128]{2,1,0:T(8,128)S(1)} %get-tuple-element.92), custom_call_target="InvertDiagBlocksLowerTriangular" | custom-call | tf_op jit(solution)/shard_map/jit(cholesky)/cholesky | solution.py:70
  369.9 11.7 %cholesky.181 = f32[128,128]{1,0:T(8,128)S(1)} custom-call(f32[128,128]{1,0:T(8,128)S(1)} %convolution_subtract_fusion.3), custom_call_target="Cholesky" | custom-call | tf_op jit(solution)/shard_map/jit(cholesky)/cholesky | solution.py:70
  385.4 153.8 %all-reduce.15.cloned.1.call-done = (f32[256,128]{1,0:T(8,128)}, f32[256,128]{1,0:T(8,128)}, f32[256,256]{1,0:T(8,128)}) async-done(((f32[256,128]{1,0:T(8,128)}, f32[256,128]{1,0:T(8,128)}, f32[256,256]{1,0:T(8,128)}), (f32[256,128]{1,0:T(8,128)}, f32[256,128]{1,0:T(8,128)}, f32[256,256]{1,0:T(8,128)})) %all-reduce.15.cloned.1.call-update) | async-done | bytes 524304 | tf_op jit(solution)/shard_map/psum | solution.py:11
  540.2 4.1 while.8
  540.8 1.4 bitcast_dynamic-update-slice_fusion.5
  542.9 1.4 bitcast_dynamic-update-slice_fusion.5
  544.3 19.7 %custom-call.17 = f32[2,128,128]{1,2,0:T(8,128)S(1)} custom-call(f32[2,128,128]{2,1,0:T(8,128)S(1)} %get-tuple-element.39), custom_call_target="InvertDiagBlocksLowerTriangular" | custom-call | tf_op jit(solution)/shard_map/triangular_solve/custom-call.0 | solution.py:17
  568.3 117.7 %all-reduce.17.cloned.1.call-done = (f32[256,128]{1,0:T(8,128)}, f32[256,128]{1,0:T(8,128)}, f32[256,128]{1,0:T(8,128)}) async-done(((f32[256,128]{1,0:T(8,128)}, f32[256,128]{1,0:T(8,128)}, f32[256,128]{1,0:T(8,128)}), (f32[256,128]{1,0:T(8,128)}, f32[256,128]{1,0:T(8,128)}, f32[256,128]{1,0:T(8,128)})) %all-reduce.17.cloned.1.call-update) | async-done | bytes 393232 | tf_op jit(solution)/shard_map/psum | solution.py:11
  685.9 1.7 broadcast_select_fusion.3
  691.0 157.0 %all-reduce.13.cloned.1.call-done = (f32[256,128]{1,0:T(8,128)}, f32[1,256,128]{2,1,0:T(8,128)}, f32[256,128]{1,0:T(8,128)}, f32[256,128]{1,0:T(8,128)}, f32[256...) async-done(((f32[256,128]{1,0:T(8,128)}, f32[1,256,128]{2,1,0:T(8,128)}, f32[256,128]{1,0:T(8,128)}, f32[256,128]{1,0:T(8,128)}, ...) | async-done | bytes 1048592 | tf_op jit(solution)/shard_map/psum | solution.py:11
  848.0 1.4 fusion.64
  854.1 1.2 fusion.4
  (115 shorter events, 28.9 us)
Async XLA Ops:
  6.5 194.2 %all-reduce.11.cloned.1.call-start = ((), (), s32[]{:S(2)}) async-start(), calls=%async_computation | async-start | bytes 524288 | tf_op jit(solution)/shard_map/psum | solution.py:11
  6.5 1.2 copy-start.3
  44.3 0.9 copy-start.10
  44.3 299.5 %all-reduce.19.cloned.1.call-start = ((), (), s32[]{:S(2)}) async-start(), calls=%async_computation.4 | async-start | bytes 524288 | tf_op jit(solution)/shard_map/psum | solution.py:11
  46.0 0.9 copy-start.4
  227.0 312.2 %all-reduce.15.cloned.1.call-start = ((), (), s32[]{:S(2)}) async-start(), calls=%async_computation.2 | async-start | bytes 1048576 | tf_op jit(solution)/shard_map/psum | solution.py:11
  343.8 1.4 copy-start
  345.3 1.0 copy-start.1
  385.1 300.8 %all-reduce.17.cloned.1.call-start = ((), (), s32[]{:S(2)}) async-start(), calls=%async_computation.3 | async-start | bytes 786432 | tf_op jit(solution)/shard_map/psum | solution.py:11
  544.3 20.0 %copy-start.2 = (f32[256,128]{1,0:T(8,128)S(1)}, f32[256,128]{1,0:T(8,128)}, u32[]{:S(2)}) copy-start(f32[256,128]{1,0:T(8,128)} %get-tuple-element.65) | copy-start | bytes 393220
  564.8 0.9 copy-start.8
  568.2 279.8 %all-reduce.13.cloned.1.call-start = ((), (), s32[]{:S(2)}) async-start(), calls=%async_computation.1 | async-start | bytes 2097152 | tf_op jit(solution)/shard_map/psum | solution.py:11
  685.9 1.7 copy-start.7
  687.6 1.0 copy-start.6
  689.7 0.9 copy-start.5
  848.0 1.4 copy-start.14
  849.4 0.9 copy-start.12
  849.4 1.0 copy-start.13
  850.4 0.9 copy-start.9
  850.4 1.0 copy-start.11
  851.3 0.9 copy-start.15
Sparse Core Ops, SparseCore 0:
  44.5 156.2 all-reduce.10
  227.2 116.6 all-reduce.18
  385.2 153.9 all-reduce.14
  568.3 117.5 all-reduce.16
  690.7 157.2 all-reduce.12
where the time goes:
time: 865 us; the launch traced here: 862 us
  waiting for transfers between devices  698 us (81%)
  other arithmetic  119 us (14%)
  between operations  16.3 us (2%)
  local copies, waits for them, and re-layouts  14.2 us (2%)
  matrix products  13.4 us (2%)
    psum x5, waiting for transfers between devices, from_root(): return lax.psum(jnp.where(mine, shard, jnp.zeros_like(shard)), axis)  698 us
    another operation x5, other arithmetic, lower_solve(): lax.linalg.triangular_solve(factor, flattened, left_side=True, lower=True)  41.3 us
    another operation x7, other arithmetic, shards(): second_pivot = from_root(jnp.linalg.cholesky(shifted), 'row', 1)  34.7 us
    another operation x6, other arithmetic, shards(): first_pivot = from_root(jnp.linalg.cholesky(diag_tiles[0]), 'row', 0)  34 us
  transfers between devices with their start and end apart: 5, of which 5 were waited for; matrix products, arithmetic and copies ran while one was open for 0% of the time, Pallas kernels for 0%

commit v1 on v0

v1 whole, which is shorter than its diff:
```python
import functools
import jax
import jax.numpy as jnp
from jax import lax
from jax.experimental import pallas as pl
from jax.experimental.pallas import tpu as pltpu
from jax.sharding import PartitionSpec as P

F32 = jnp.float32
MESH = pl.DeviceIdType.MESH


def across(v, k):
    return jnp.broadcast_to(v[:, k:k + 1], (8, 128))


def down(v, k):
    return jnp.broadcast_to(v[k:k + 1, :], (8, 128))


def inverse_factor(S):
    n = 16
    row = lax.broadcasted_iota(jnp.int32, (8, 128), 0)
    lane = lax.broadcasted_iota(jnp.int32, (8, 128), 1)
    R = [S[8 * i:8 * i + 8, :] for i in range(n)]
    E = [jnp.where(lane == row + 8 * i, 1.0, 0.0).astype(F32) for i in range(n)]
    out = []
    here = [across(R[0], j) for j in range(8)]
    for K in range(n):
        last = K == n - 1
        rk, ek = R[K], E[K]
        if not last:
            below = [across(R[K + 1], 8 * K + j) for j in range(8)]
            below_old = list(below)
            after = [across(R[K + 1], 8 * K + 8 + j) for j in range(8)]
        lin = jnp.zeros((8, 128), F32)
        for k in range(8):
            p = down(here[k], k)
            r = 1.0 / p
            rs = lax.rsqrt(p)
            isk = row == k
            erow = down(ek, k)
            lin = jnp.where(isk, erow * rs, lin)
            if last:
                if k < 7:
                    m = here[k] * r
                    ek = ek - m * erow
                    for j in range(k + 1, 8):
                        here[j] = here[j] - m * down(here[k], j)
                continue
            m = jnp.where(isk, 0.0, here[k] * r)
            m1 = below[k] * r
            rrow = down(rk, k)
            f = jnp.where(isk, r, 1.0)
            rk = rk * f - m * rrow
            ek = ek * f - m * erow
            for j in range(k + 1, 8):
                here[j] = here[j] * f - m * down(here[k], j)
            for j in range(8):
                after[j] = after[j] - m1 * down(below[k], j)
            for j in range(k + 1, 8):
                below[j] = below[j] - m1 * down(here[k], j)
        out.append(lin)
        if not last:
            z = [down(rk, k) for k in range(8)]
            ze = [down(ek, k) for k in range(8)]
            for I in range(K + 1, n):
                c = below_old if I == K + 1 else [across(R[I], 8 * K + j) for j in range(8)]
                a, b = R[I], E[I]
                for k in range(8):
                    a = a - c[k] * z[k]
                    b = b - c[k] * ze[k]
                R[I], E[I] = a, b
            here = after
    return jnp.concatenate(out, axis=0)


def nt(a, b):
    return lax.dot_general(a, b, (((1,), (1,)), ((), ())),
                           precision=lax.Precision.HIGHEST, preferred_element_type=F32)


def front_tile(left, right, rank):
    live = lax.broadcasted_iota(jnp.int32, left.shape, 1) < rank
    left = jnp.where(live, left.astype(F32), 0.0).astype(jnp.bfloat16)
    return lax.dot_general(left, right, (((1,), (1,)), ((), ())), preferred_element_type=F32)


class Traffic:
    def __init__(self, diag, a, d00, d11, b10, col, rowb, scratch):
        self.diag, self.a = diag, a
        self.d00, self.d11, self.b10, self.col, self.rowb = d00, d11, b10, col, rowb
        (self.d00p, self.d11p, self.b10p, self.pbuf, self.colz, self.colp, self.ss, self.rs) = scratch
        self.row = lax.axis_index("row")
        self.c = lax.axis_index("col")
        self.z = self.c // 2
        self.k = lax.rem(self.c, 2)
        self.later = []

    def remote(self, src, dst, g, **to):
        return pltpu.make_async_remote_copy(src, dst, self.ss.at[g], self.rs.at[g],
                                            device_id=to, device_id_type=MESH)

    def local(self, src, dst, g):
        pltpu.make_async_copy(src, dst, self.rs.at[g]).start()

    def arrived(self, ref, g):
        pltpu.make_async_copy(ref, ref, self.rs.at[g]).wait()

    def loop(self, n, body):
        def step(d, carry):
            body(d)
            return carry
        lax.fori_loop(1, n, step, 0)

    def run(self, cond, work):
        if cond is None:
            work(lambda copy: copy.start())
            self.later.append(lambda: work(lambda copy: copy.wait_send()))
        else:
            pl.when(cond)(lambda: work(lambda copy: copy.start()))
            self.later.append(lambda: pl.when(cond)(lambda: work(lambda copy: copy.wait_send())))

    def to_rows(self, src, dst, g, pred=None):
        def work(act):
            def one(d):
                q = lax.rem(self.row + d, 32)
                copy = self.remote(src(q), dst, g, row=q)
                if pred is None:
                    act(copy)
                else:
                    pl.when(pred(q))(lambda: act(copy))
            self.loop(32, one)
        return work

    def barrier(self):
        bar = pltpu.get_barrier_semaphore()

        def greet(**to):
            pl.semaphore_signal(bar, inc=1, device_id=to, device_id_type=MESH)
        self.loop(32, lambda d: greet(row=lax.rem(self.row + d, 32)))
        self.loop(8, lambda d: greet(col=lax.rem(self.z + d, 8) * 2 + self.k))
        greet(col=self.z * 2 + 1 - self.k)
        pl.semaphore_wait(bar, 39)

    def scatter_diag(self):
        for root, piece, g in ((0, self.d00p, 0), (1, self.d11p, 1)):
            mine = self.row == root
            self.run(mine, self.to_rows(lambda q: self.diag.at[0, pl.ds(pl.multiple_of(8 * q, 8), 8), :], piece, g))
            pl.when(mine)(functools.partial(self.local, self.diag.at[0, pl.ds(8 * root, 8), :], piece, g))

    def gather(self, piece, whole, pg, g):
        self.arrived(piece, pg)
        self.run(None, self.to_rows(lambda q: piece, whole.at[self.row], g))
        self.local(piece, whole.at[self.row], g)

    def scatter_front(self):
        a, home = self.a.at[0], self.z == 0
        self.run(home, self.to_rows(lambda q: a.at[pl.ds(pl.multiple_of(8 * q, 8), 8), :], self.pbuf.at[self.row], 2))

        def along(act):
            def one(zz):
                there = dict(col=2 * zz + self.k)
                rows = pl.ds(pl.multiple_of(32 * zz, 32), 32)
                act(self.remote(a.at[rows, :], self.rowb.at[self.k, rows, :], 3, **there))
                act(self.remote(a.at[pl.ds(0, 32), :], self.rowb.at[self.k, pl.ds(0, 32), :], 4, **there))
            self.loop(8, one)
        self.run(home, along)

        @pl.when(home)
        def _():
            self.local(a.at[pl.ds(pl.multiple_of(8 * self.row, 8), 8), :], self.pbuf.at[self.row], 2)
            self.local(a, self.rowb.at[self.k], 4)

    def front_to_planes(self):
        home = self.z == 0

        @pl.when(home)
        def _():
            self.arrived(self.pbuf, 2)

        def work(act):
            def one(zz):
                there = dict(col=2 * zz + self.k)

                @pl.when(self.k == 0)
                def _():
                    act(self.remote(self.pbuf.at[1], self.b10p, 5, **there))
                for t in range(2):
                    act(self.remote(self.pbuf.at[pl.ds(2 * zz + 16 * t, 2)], self.colz.at[t], 6, **there))
            self.loop(8, one)
        self.run(home, work)

        @pl.when(home)
        def _():
            for t in range(2):
                self.local(self.pbuf.at[pl.ds(16 * t, 2)], self.colz.at[t], 6)
            pl.when(self.k == 0)(lambda: self.local(self.pbuf.at[1], self.b10p, 5))

    def rows_along(self):
        away = self.z > 0
        mine = pl.ds(pl.multiple_of(32 * self.z, 32), 32)
        held = self.rowb.at[self.k]

        @pl.when(away)
        def _():
            self.arrived(held.at[mine, :], 3)

        def work(act):
            def one(d):
                zz = 1 + lax.rem(self.z - 1 + d, 7)
                act(self.remote(held.at[mine, :], held.at[mine, :], 4, col=2 * zz + self.k))
            self.loop(7, one)
        self.run(away, work)

    def rows_across(self):
        held = self.rowb.at[self.k]
        pl.when(self.z > 0)(lambda: self.arrived(held.at[pl.ds(0, 224), :], 4))
        pl.when(self.z == 0)(lambda: self.arrived(held, 4))
        self.run(None, lambda act: act(self.remote(held, held, 7, col=self.z * 2 + 1 - self.k)))

    def rows_done(self):
        self.arrived(self.rowb.at[1 - self.k], 7)

    def across_cores(self):
        sibling = dict(col=self.z * 2 + 1 - self.k)
        pl.when(self.k == 0)(lambda: self.arrived(self.b10p, 5))
        self.run(self.k == 0, lambda act: act(self.remote(self.b10p, self.b10p, 5, **sibling)))
        self.arrived(self.colz, 6)

        def work(act):
            for t in range(2):
                act(self.remote(self.colz.at[t, 1 - self.k], self.colp.at[t, self.k], 8, **sibling))
        self.run(None, work)
        for t in range(2):
            self.local(self.colz.at[t, self.k], self.colp.at[t, self.k], 8)

    def gather_b10(self):
        pl.when(self.k == 1)(lambda: self.arrived(self.b10p, 5))
        self.run(None, self.to_rows(lambda q: self.b10p, self.b10.at[self.row], 9))
        self.local(self.b10p, self.b10.at[self.row], 9)

    def needs(self, q, t):
        below = q > self.c + 16 * t
        return jnp.logical_and(below, self.c >= 2) if t == 0 else below

    def gather_cols(self):
        self.arrived(self.colp, 8)
        for t in range(2):
            dst = self.col.at[t, :, self.row]
            self.run(None, self.to_rows(lambda q, t=t: self.colp.at[t], dst, 12 + t, lambda q, t=t: self.needs(q, t)))
            pl.when(self.needs(self.row, t))(functools.partial(self.local, self.colp.at[t], dst, 12 + t))

    def cols_done(self):
        for t in range(2):
            pl.when(self.needs(self.row, t))(functools.partial(self.arrived, self.col.at[t], 12 + t))

    def finish(self):
        for wait in self.later:
            wait()


def own_tiles(ranks, left, right, a):
    r, c = lax.axis_index("row"), lax.axis_index("col")
    for t in range(2):
        a[t] = front_tile(left[0, t], right[0, t], ranks[r, c + 16 * t])


def whole(ref):
    return ref[...].reshape(256, 256)


def panels(d00, d11, b10, col, rowb, a, out, at):
    H = 128
    r, c = lax.axis_index("row"), lax.axis_index("col")
    at("d00")
    A = whole(d00)
    L1 = inverse_factor(A[:H, :H])
    at("one")
    T1 = nt(A[H:, :H], L1)
    L2 = inverse_factor(A[H:, H:] - nt(T1, T1))
    at("b10")
    B = whole(b10)

    def first(B):
        Fa = nt(B[:, :H], L1)
        return Fa, nt(B[:, H:] - nt(Fa, T1), L2)
    Fa, Fb = first(B)
    at("d11")
    M = whole(d11)
    L3 = inverse_factor(M[:H, :H] - nt(Fa[:H], Fa[:H]) - nt(Fb[:H], Fb[:H]))
    at("three")
    M21 = M[H:, :H] - nt(Fa[H:], Fa[:H]) - nt(Fb[H:], Fb[:H])
    T3 = nt(M21, L3)
    L4 = inverse_factor(M[H:, H:] - nt(Fa[H:], Fa[H:]) - nt(Fb[H:], Fb[H:]) - nt(T3, T3))
    at("tiles")

    def both(b0, b1):
        xa, xb = first(b0)
        C = b1 - nt(xa, Fa) - nt(xb, Fb)
        ya = nt(C[:, :H], L3)
        yb = nt(C[:, H:] - nt(ya, T3), L4)
        return [jnp.concatenate(p, axis=1) for p in ((xa, xb), (ya, yb))]
    X, Y = both(rowb[0], rowb[1])
    for t in range(2):
        j = c + 16 * t
        Xj, Yj = both(whole(col.at[t, 0]), whole(col.at[t, 1]))
        value = a[t] - nt(X, Xj) - nt(Y, Yj)
        if t == 0:
            value = jnp.where(j == 0, X, jnp.where(j == 1, Y, value))
        out[0, t] = jnp.where(j < r, value, 0.0)


def comm_scratch():
    V = pltpu.VMEM
    return [V((8, 256), F32), V((8, 256), F32), V((8, 256), F32), V((32, 8, 256), F32),
            V((2, 2, 8, 256), F32), V((2, 2, 8, 256), F32),
            pltpu.SemaphoreType.DMA((14,)), pltpu.SemaphoreType.DMA((14,))]


LAND = [(32, 8, 256), (32, 8, 256), (32, 8, 256), (2, 2, 32, 8, 256), (2, 256, 256)]


def send_kernel(ranks, diag, left, right, d00, d11, b10, col, rowb, a, *scratch):
    own_tiles(ranks, left, right, a)
    t = Traffic(diag, a, d00, d11, b10, col, rowb, scratch)
    t.barrier()
    t.scatter_diag()
    t.scatter_front()
    t.gather(t.d00p, t.d00, 0, 10)
    t.gather(t.d11p, t.d11, 1, 11)
    t.rows_along()
    t.front_to_planes()
    t.across_cores()
    t.gather_b10()
    t.gather_cols()
    t.rows_across()
    t.rows_done()
    t.arrived(t.d00, 10)
    t.arrived(t.d11, 11)
    t.arrived(t.b10, 9)
    t.cols_done()
    t.finish()


def chain_kernel(d00, d11, b10, col, rowb, a, out):
    panels(d00, d11, b10, col, rowb, a, out, lambda name: None)


def shards(diag, left, right, ranks):
    vmem = pl.BlockSpec(memory_space=pltpu.VMEM)
    landed = pl.pallas_call(
        send_kernel,
        out_shape=[jax.ShapeDtypeStruct(s, F32) for s in LAND + [(2, 256, 256)]],
        in_specs=[pl.BlockSpec(memory_space=pltpu.SMEM), pl.BlockSpec(memory_space=pl.ANY), vmem, vmem],
        out_specs=[vmem] * 6,
        scratch_shapes=comm_scratch(),
        compiler_params=pltpu.CompilerParams(collective_id=0, has_side_effects=True, vmem_limit_bytes=32 << 20),
    )(ranks, diag, left, right)
    return pl.pallas_call(
        chain_kernel,
        out_shape=jax.ShapeDtypeStruct((1, 2, 256, 256), F32),
        in_specs=[vmem] * 6,
        out_specs=vmem,
        compiler_params=pltpu.CompilerParams(vmem_limit_bytes=32 << 20),
    )(*landed)


def solution(mesh):
    in_specs = (P("row", None, None), P("row", "col", None, None), P("row", "col", None, None), P())
    return jax.shard_map(shards, mesh=mesh, in_specs=in_specs, out_specs=P("row", "col", None, None), check_vma=False)
```

time: 865 us -> 83.2 us (0.10)
  the two profiles are of different devices: /device:TPU:1 before, /device:TPU:121 now
where the time goes in v1:
time: 83.2 us; the launch traced here: 83 us
  Pallas kernels  79.5 us (96%)
  local copies, waits for them, and re-layouts  3.47 us (4%)
    pallas_call x1, Pallas kernels, shards(): pl.pallas_call(send_kernel, out_shape=[jax.ShapeDtypeStruct(s, F32) for s...  58.2 us
    pallas_call x1, Pallas kernels, shards(): pl.pallas_call(chain_kernel, out_shape=jax.ShapeDtypeStruct((1, 2, 256, 2...  21.3 us
    unnamed x8, local copies, waits for them, and re-layouts  3.47 us

profile of v1, /device:TPU:121, one launch (start us, length us, event | category | flops | bytes accessed | tf_op | source)
XLA Modules:
  0.0 83.0 jit_solution(8047033568286585637)
XLA Ops:
  0.0 0.0 copy-start
  0.0 0.9 %copy-done = f32[1,256,256]{2,1,0:T(8,128)S(1)} copy-done((f32[1,256,256]{2,1,0:T(8,128)S(1)}, f32[1,256,256]{2,1,0:T(8,128)}, u32[]{:S(2)}) %copy-start) | copy-done | bytes 262168
  1.0 0.0 copy-start.1
  1.0 0.9 %copy-done.1 = bf16[1,2,256,128]{3,2,1,0:T(8,128)(2,1)S(1)} copy-done((bf16[1,2,256,128]{3,2,1,0:T(8,128)(2,1)S(1)}, bf16[1,2,256,128]{3,2,1,0:T(8,128)(2,1)}, u32[]{:S(2)}) %copy-start.1) | copy-done | bytes 131096
  1.9 0.0 copy-start.2
  1.9 0.9 %copy-done.2 = bf16[1,2,256,128]{3,2,1,0:T(8,128)(2,1)S(1)} copy-done((bf16[1,2,256,128]{3,2,1,0:T(8,128)(2,1)S(1)}, bf16[1,2,256,128]{3,2,1,0:T(8,128)(2,1)}, u32[]{:S(2)}) %copy-start.2) | copy-done | bytes 131096
  2.8 0.0 copy-start.3
  2.8 0.7 copy-done.3
  3.5 58.2 %shard_map.46 = (f32[32,8,256]{2,1,0:T(8,128)S(1)}, f32[32,8,256]{2,1,0:T(8,128)S(1)}, f32[32,8,256]{2,1,0:T(8,128)S(1)}, f32[2,2,32,8,256]{4,3,2,1,0:T(8,128)S(...) custom-call(s32[32,32]{1,0:T(8,128)S(1)} %copy-done.3, f32[1,256,256]{2,1,0:T(8,128)S(1)} %copy-done, ...), custom_call_target="tpu_custom_call" | custom-call | tf_op jit(solution)/shard_map/pallas_call | solution.py:352
  61.6 21.3 %shard_map.47 = f32[1,2,256,256]{3,2,1,0:T(8,128)} custom-call(f32[32,8,256]{2,1,0:T(8,128)S(1)} %get-tuple-element.11.d00, f32[32,8,256]{2,1,0:T(8,128)S(1)} %get-tuple-element.12.d11, f32[32,8,256]{2,1,0:T(8,128)S(1)} %get-tuple-element.13.b10, f32[2,2,32,8,256]{4,3,2,1,0:T(8,128)S(1)} %get-tuple-element.14.col, ...), custom_call_target="tpu_custom_call" | custom-call | tf_op jit(solution)/shard_map/pallas_call | solution.py:360
Async XLA Ops:
  0.0 0.9 %copy-start = (f32[1,256,256]{2,1,0:T(8,128)S(1)}, f32[1,256,256]{2,1,0:T(8,128)}, u32[]{:S(2)}) copy-start(f32[1,256,256]{2,1,0:T(8,128)} %diag.1) | copy-start | bytes 786436
  1.0 0.9 %copy-start.1 = (bf16[1,2,256,128]{3,2,1,0:T(8,128)(2,1)S(1)}, bf16[1,2,256,128]{3,2,1,0:T(8,128)(2,1)}, u32[]{:S(2)}) copy-start(bf16[1,2,256,128]{3,2,1,0:T(8,128)(2,1)} %left.1) | copy-start | bytes 393220
  1.9 0.9 %copy-start.2 = (bf16[1,2,256,128]{3,2,1,0:T(8,128)(2,1)S(1)}, bf16[1,2,256,128]{3,2,1,0:T(8,128)(2,1)}, u32[]{:S(2)}) copy-start(bf16[1,2,256,128]{3,2,1,0:T(8,128)(2,1)} %right.1) | copy-start | bytes 393220
  2.8 0.7 copy-start.3

commit v2 on v1

v2 whole, which is shorter than its diff:
```python
import functools
import jax
import jax.numpy as jnp
from jax import lax
from jax.experimental import pallas as pl
from jax.experimental.pallas import tpu as pltpu
from jax.sharding import PartitionSpec as P

F32 = jnp.float32
MESH = pl.DeviceIdType.MESH


def across(v, k):
    return jnp.broadcast_to(v[:, k:k + 1], (8, 128))


def down(v, k):
    return jnp.broadcast_to(v[k:k + 1, :], (8, 128))


def inverse_factor(S, at=lambda block: None):
    n = 16
    row = lax.broadcasted_iota(jnp.int32, (8, 128), 0)
    lane = lax.broadcasted_iota(jnp.int32, (8, 128), 1)
    R = [S[8 * i:8 * i + 8, :] for i in range(n)]
    E = [jnp.where(lane == row + 8 * i, 1.0, 0.0).astype(F32) for i in range(n)]
    out = []
    here = [across(R[0], j) for j in range(8)]
    for K in range(n):
        at(K)
        last = K == n - 1
        rk, ek = R[K], E[K]
        if not last:
            below = [across(R[K + 1], 8 * K + j) for j in range(8)]
            below_old = list(below)
            after = [across(R[K + 1], 8 * K + 8 + j) for j in range(8)]
        lin = jnp.zeros((8, 128), F32)
        for k in range(8):
            p = down(here[k], k)
            r = 1.0 / p
            rs = lax.rsqrt(p)
            isk = row == k
            erow = down(ek, k)
            lin = jnp.where(isk, erow * rs, lin)
            if last:
                if k < 7:
                    m = here[k] * r
                    ek = ek - m * erow
                    for j in range(k + 1, 8):
                        here[j] = here[j] - m * down(here[k], j)
                continue
            m = jnp.where(isk, 0.0, here[k] * r)
            m1 = below[k] * r
            rrow = down(rk, k)
            f = jnp.where(isk, r, 1.0)
            rk = rk * f - m * rrow
            ek = ek * f - m * erow
            for j in range(k + 1, 8):
                here[j] = here[j] * f - m * down(here[k], j)
            for j in range(8):
                after[j] = after[j] - m1 * down(below[k], j)
            for j in range(k + 1, 8):
                below[j] = below[j] - m1 * down(here[k], j)
        out.append(lin)
        if not last:
            z = [down(rk, k) for k in range(8)]
            ze = [down(ek, k) for k in range(8)]
            for I in range(K + 1, n):
                c = below_old if I == K + 1 else [across(R[I], 8 * K + j) for j in range(8)]
                a, b = R[I], E[I]
                for k in range(8):
                    a = a - c[k] * z[k]
                    b = b - c[k] * ze[k]
                R[I], E[I] = a, b
            here = after
    return jnp.concatenate(out, axis=0)


def nt(a, b):
    return lax.dot_general(a, b, (((1,), (1,)), ((), ())),
                           precision=lax.Precision.HIGHEST, preferred_element_type=F32)


def front_tile(left, right, rank):
    live = lax.broadcasted_iota(jnp.int32, left.shape, 1) < rank
    left = jnp.where(live, left.astype(F32), 0.0).astype(jnp.bfloat16)
    return lax.dot_general(left, right, (((1,), (1,)), ((), ())), preferred_element_type=F32)


class Traffic:
    def __init__(self, diag, a, bufs, sems):
        self.diag, self.a = diag, a
        (self.d00, self.dd, self.b10, self.col, self.rowb,
         self.d00p, self.ddp, self.b10p, self.pbuf, self.colz, self.colp) = bufs
        self.ss, self.rs = sems
        self.row = lax.axis_index("row")
        self.c = lax.axis_index("col")
        self.y, self.x = self.row // 4, lax.rem(self.row, 4)
        self.z, self.k = self.c // 2, lax.rem(self.c, 2)
        self.other = dict(col=self.z * 2 + 1 - self.k)
        self.later = []

    def remote(self, src, dst, g, **to):
        return pltpu.make_async_remote_copy(src, dst, self.ss.at[g], self.rs.at[g],
                                            device_id=to, device_id_type=MESH)

    def local(self, src, dst, g):
        pltpu.make_async_copy(src, dst, self.rs.at[g]).start()

    def arrived(self, ref, g):
        pltpu.make_async_copy(ref, ref, self.rs.at[g]).wait()

    def loop(self, lo, hi, body):
        def step(d, carry):
            body(d)
            return carry
        lax.fori_loop(lo, hi, step, 0)

    def run(self, cond, work):
        if cond is None:
            work(lambda copy: copy.start())
            self.later.append(lambda: work(lambda copy: copy.wait_send()))
        else:
            pl.when(cond)(lambda: work(lambda copy: copy.start()))
            self.later.append(lambda: pl.when(cond)(lambda: work(lambda copy: copy.wait_send())))

    def barrier(self):
        bar = pltpu.get_barrier_semaphore()

        def greet(**to):
            pl.semaphore_signal(bar, inc=1, device_id=to, device_id_type=MESH)
        self.loop(1, 32, lambda d: greet(row=lax.rem(self.row + d, 32)))
        self.loop(1, 8, lambda d: greet(col=lax.rem(self.z + d, 8) * 2 + self.k))
        greet(**self.other)
        pl.semaphore_wait(bar, 39)

    def scatter(self, cond, src, dst, g):
        def work(act):
            def one(d):
                q = lax.rem(self.row + d, 32)
                act(self.remote(src(8 * lax.rem(q, 4) + q // 4), dst, g, row=q))
            self.loop(1, 32, one)
        self.run(cond, work)
        pl.when(cond)(lambda: self.local(src(8 * self.x + self.y), dst, g))

    def block(self, rows, half):
        return self.diag.at[0, pl.ds(pl.multiple_of(rows, 8), 8), pl.ds(128 * half, 128)]

    def scatter_diag(self):
        self.scatter(self.row == 0, lambda g: self.block(8 * g, 0), self.d00p, 0)

    def scatter_rest(self):
        for root, k, lo, rows, half in ((0, 0, 0, 128, 1), (1, 0, 16, 0, 0), (1, 1, 0, 128, 0), (1, 1, 16, 128, 1)):
            mine = jnp.logical_and(self.row == root, self.k == k)

            def work(act, root=root, lo=lo, rows=rows, half=half):
                def one(i):
                    g = lo + i
                    q = 4 * lax.rem(g, 8) + g // 8
                    src = self.block(rows + 8 * i, half)
                    pl.when(q != root)(lambda: act(self.remote(src, self.ddp, 1, row=q)))
                self.loop(0, 16, one)
            self.run(mine, work)
            own = 8 * root - lo
            if 0 <= own < 16:
                pl.when(mine)(lambda: self.local(self.block(rows + 8 * own, half), self.ddp, 1))

    def along_y(self, piece, whole, pg, g, pred=None):
        self.arrived(piece, pg)
        dst = whole.at[self.x, self.y]

        def work(act):
            def one(d):
                y = lax.rem(self.y + d, 8)
                copy = self.remote(piece, dst, g, row=4 * y + self.x)
                if pred is None:
                    act(copy)
                else:
                    pl.when(pred(y))(lambda: act(copy))
            self.loop(1, 8, one)
        self.run(None, work)
        mine = lambda: self.local(piece, dst, g)
        mine() if pred is None else pl.when(pred(self.y))(mine)

    def along_x(self, whole, g, pred=None, line=None):
        held = whole.at[self.x]
        here = lambda: self.arrived(held, g)
        here() if line is None else pl.when(line(self.y))(here)

        def work(act):
            for d in (1, 3, 2):
                x = lax.rem(self.x + d, 4)
                copy = self.remote(held, held, g + 1, row=4 * self.y + x)
                if pred is None:
                    act(copy)
                else:
                    pl.when(pred(4 * self.y + x))(functools.partial(act, copy))
        self.run(None, work)

    def all_here(self, whole, g):
        self.arrived(whole.at[pl.ds(0, 3)], g + 1)

    def to_other_core(self, whole, g):
        self.all_here(whole.at[self.k], g)
        self.run(None, lambda act: act(self.remote(whole.at[self.k], whole.at[self.k], g + 2, **self.other)))

    def from_other_core(self, whole, g):
        self.arrived(whole.at[1 - self.k], g + 2)

    def scatter_front(self):
        a, home = self.a.at[0], self.z == 0
        self.scatter(home, lambda g: a.at[pl.ds(pl.multiple_of(8 * g, 8), 8), :], self.pbuf.at[self.row], 2)

    def scatter_rows(self):
        a, home = self.a.at[0], self.z == 0

        def along(act):
            def one(zz):
                there = dict(col=2 * zz + self.k)
                rows = pl.ds(pl.multiple_of(32 * zz, 32), 32)
                act(self.remote(a.at[rows, :], self.rowb.at[self.k, rows, :], 3, **there))
                act(self.remote(a.at[pl.ds(0, 32), :], self.rowb.at[self.k, pl.ds(0, 32), :], 4, **there))
            self.loop(1, 8, one)
        self.run(home, along)
        pl.when(home)(lambda: self.local(a, self.rowb.at[self.k], 4))

    def front_to_planes(self):
        home = self.z == 0
        pl.when(home)(lambda: self.arrived(self.pbuf, 2))

        def work(act):
            def one(zz):
                there = dict(col=2 * zz + self.k)

                @pl.when(self.k == 0)
                def _():
                    act(self.remote(self.pbuf.at[1], self.b10p, 5, **there))
                for t in range(2):
                    act(self.remote(self.pbuf.at[pl.ds(2 * zz + 16 * t, 2)], self.colz.at[t], 6, **there))
            self.loop(1, 8, one)
        self.run(home, work)

        @pl.when(home)
        def _():
            for t in range(2):
                self.local(self.pbuf.at[pl.ds(16 * t, 2)], self.colz.at[t], 6)
            pl.when(self.k == 0)(lambda: self.local(self.pbuf.at[1], self.b10p, 5))

    def rows_along(self):
        away = self.z > 0
        mine = pl.ds(pl.multiple_of(32 * self.z, 32), 32)
        held = self.rowb.at[self.k]
        pl.when(away)(lambda: self.arrived(held.at[mine, :], 3))

        def work(act):
            def one(d):
                zz = 1 + lax.rem(self.z - 1 + d, 7)
                act(self.remote(held.at[mine, :], held.at[mine, :], 4, col=2 * zz + self.k))
            self.loop(1, 7, one)
        self.run(away, work)

    def rows_across(self):
        held = self.rowb.at[self.k]
        pl.when(self.z > 0)(lambda: self.arrived(held.at[pl.ds(0, 224), :], 4))
        pl.when(self.z == 0)(lambda: self.arrived(held, 4))
        self.run(None, lambda act: act(self.remote(held, held, 7, **self.other)))

    def rows_done(self):
        self.arrived(self.rowb.at[1 - self.k], 7)

    def b10_to_other_core(self):
        pl.when(self.k == 0)(lambda: self.arrived(self.b10p, 5))
        self.run(self.k == 0, lambda act: act(self.remote(self.b10p, self.b10p, 5, **self.other)))

    def cols_to_other_core(self):
        self.arrived(self.colz, 6)

        def work(act):
            for t in range(2):
                act(self.remote(self.colz.at[t, 1 - self.k], self.colp.at[t, self.k], 8, **self.other))
        self.run(None, work)
        for t in range(2):
            self.local(self.colz.at[t, self.k], self.colp.at[t, self.k], 8)

    def b10_along_y(self):
        pl.when(self.k == 1)(lambda: self.arrived(self.b10p, 5))
        half = self.b10p.at[:, pl.ds(pl.multiple_of(128 * self.k, 128), 128)]
        dst = self.b10.at[self.k, self.x, self.y]
        self.run(None, lambda act: self.loop(1, 8, lambda d: act(
            self.remote(half, dst, 9, row=4 * lax.rem(self.y + d, 8) + self.x))))
        self.local(half, dst, 9)

    def needs(self, q, t):
        below = q > self.c + 16 * t
        return jnp.logical_and(below, self.c >= 2) if t == 0 else below

    def line_needs(self, y, t):
        return self.needs(4 * y + 3, t)

    def cols_along_y(self):
        self.arrived(self.colp, 8)
        for t in range(2):
            piece, dst, g = self.colp.at[t], self.col.at[t, self.x, self.y], 12 + 2 * t

            def work(act, t=t, piece=piece, dst=dst, g=g):
                def one(d):
                    y = lax.rem(self.y + d, 8)
                    pl.when(self.line_needs(y, t))(lambda: act(self.remote(piece, dst, g, row=4 * y + self.x)))
                self.loop(1, 8, one)
            self.run(None, work)
            pl.when(self.line_needs(self.y, t))(functools.partial(self.local, piece, dst, g))

    def cols_along_x(self):
        for t in range(2):
            self.along_x(self.col.at[t], 12 + 2 * t, functools.partial(self.needs, t=t),
                         functools.partial(self.line_needs, t=t))

    def cols_done(self):
        for t in range(2):
            pl.when(self.needs(self.row, t))(functools.partial(self.all_here, self.col.at[t], 12 + 2 * t))

    def finish(self):
        for wait in self.later:
            wait()


def own_tiles(ranks, left, right, a):
    r, c = lax.axis_index("row"), lax.axis_index("col")
    for t in range(2):
        a[t] = front_tile(left[0, t], right[0, t], ranks[r, c + 16 * t])


def panels(net, out, at):
    H = 128
    r, c = lax.axis_index("row"), lax.axis_index("col")
    a = net.a

    def place(name):
        return lambda block: at(name, block)
    at("d00", 0)
    A = net.d00[...].reshape(256, H)
    L1 = inverse_factor(A[:H], place("first"))
    at("a22", 0)
    U0 = net.dd[0].reshape(256, H)
    T1 = nt(A[H:], L1)
    L2 = inverse_factor(U0[:H] - nt(T1, T1), place("second"))
    at("b10", 0)
    B0, B1 = net.b10[0].reshape(256, H), net.b10[1].reshape(256, H)

    def first(B0, B1):
        Fa = nt(B0, L1)
        return Fa, nt(B1 - nt(Fa, T1), L2)
    Fa, Fb = first(B0, B1)
    U1 = net.dd[1].reshape(256, H)
    L3 = inverse_factor(U0[H:] - nt(Fa[:H], Fa[:H]) - nt(Fb[:H], Fb[:H]), place("third"))
    M21 = U1[:H] - nt(Fa[H:], Fa[:H]) - nt(Fb[H:], Fb[:H])
    T3 = nt(M21, L3)
    L4 = inverse_factor(U1[H:] - nt(Fa[H:], Fa[H:]) - nt(Fb[H:], Fb[H:]) - nt(T3, T3), place("fourth"))
    at("tiles", 0)

    def both(b0, b1):
        xa, xb = first(b0[:, :H], b0[:, H:])
        C = b1 - nt(xa, Fa) - nt(xb, Fb)
        ya = nt(C[:, :H], L3)
        yb = nt(C[:, H:] - nt(ya, T3), L4)
        return [jnp.concatenate(p, axis=1) for p in ((xa, xb), (ya, yb))]
    X, Y = both(net.rowb[0], net.rowb[1])
    for t in range(2):
        j = c + 16 * t
        Xj, Yj = both(net.col[t, :, :, 0].reshape(256, 256), net.col[t, :, :, 1].reshape(256, 256))
        value = a[t] - nt(X, Xj) - nt(Y, Yj)
        if t == 0:
            value = jnp.where(j == 0, X, jnp.where(j == 1, Y, value))
        out[0, t] = jnp.where(j < r, value, 0.0)


LAND = [(4, 8, 8, 128), (2, 4, 8, 8, 128), (2, 4, 8, 8, 128), (2, 4, 8, 2, 8, 256), (2, 256, 256)]
PIECES = [(8, 128), (8, 128), (8, 256), (32, 8, 256), (2, 2, 8, 256), (2, 2, 8, 256)]


def kernel(ranks, diag, left_hbm, right_hbm, out, left, right, a, *scratch):
    bufs, (ss, rs, ls) = scratch[:11], scratch[11:]
    loads = [pltpu.make_async_copy(left_hbm, left, ls.at[0]), pltpu.make_async_copy(right_hbm, right, ls.at[1])]
    for load in loads:
        load.start()
    t = Traffic(diag, a, bufs, (ss, rs))
    t.barrier()
    t.scatter_diag()
    for load in loads:
        load.wait()
    own_tiles(ranks, left, right, a)
    t.scatter_rest()
    t.along_y(t.d00p, t.d00, 0, 16)
    t.scatter_front()
    t.along_x(t.d00, 16)
    t.scatter_rows()
    t.along_y(t.ddp, t.dd.at[t.k], 1, 18)
    stages = {
        ("d00", 0): [lambda: t.all_here(t.d00, 16)],
        ("first", 6): [lambda: t.along_x(t.dd.at[t.k], 18), t.rows_along],
        ("first", 11): [t.front_to_planes, lambda: t.to_other_core(t.dd, 18)],
        ("a22", 0): [lambda: t.from_other_core(t.dd, 18)],
        ("second", 3): [t.b10_to_other_core, t.cols_to_other_core],
        ("second", 7): [t.b10_along_y, t.cols_along_y],
        ("second", 12): [lambda: t.along_x(t.b10.at[t.k], 9)],
        ("b10", 0): [lambda: t.to_other_core(t.b10, 9), t.cols_along_x, lambda: t.from_other_core(t.b10, 9)],
        ("third", 8): [t.rows_across],
        ("tiles", 0): [t.rows_done, t.cols_done],
    }

    def at(name, block):
        for stage in stages.get((name, block), []):
            stage()
    panels(t, out, at)
    t.finish()


def shards(diag, left, right, ranks):
    hbm = pl.BlockSpec(memory_space=pl.ANY)
    V = pltpu.VMEM
    return pl.pallas_call(
        kernel,
        out_shape=jax.ShapeDtypeStruct((1, 2, 256, 256), F32),
        in_specs=[pl.BlockSpec(memory_space=pltpu.SMEM), hbm, hbm, hbm],
        out_specs=pl.BlockSpec(memory_space=pltpu.VMEM),
        scratch_shapes=[V((1, 2, 256, 128), jnp.bfloat16), V((1, 2, 256, 128), jnp.bfloat16), V((2, 256, 256), F32)]
        + [V(s, F32) for s in LAND + PIECES]
        + [pltpu.SemaphoreType.DMA((21,)), pltpu.SemaphoreType.DMA((21,)), pltpu.SemaphoreType.DMA((2,))],
        compiler_params=pltpu.CompilerParams(collective_id=0, has_side_effects=True, vmem_limit_bytes=60 << 20),
    )(ranks, diag, left, right)


def solution(mesh):
    in_specs = (P("row", None, None), P("row", "col", None, None), P("row", "col", None, None), P())
    return jax.shard_map(shards, mesh=mesh, in_specs=in_specs, out_specs=P("row", "col", None, None), check_vma=False)
```

time: 83.2 us -> 66.8 us (0.80)
  the two profiles are of different devices: /device:TPU:121 before, /device:TPU:1 now
where the time goes in v2:
time: 66.8 us; the launch traced here: 66.5 us
  Pallas kernels  64.6 us (97%)
  local copies, waits for them, and re-layouts  1.87 us (3%)
    pallas_call x1, Pallas kernels, shards(): pl.pallas_call(kernel, out_shape=jax.ShapeDtypeStruct((1, 2, 256, 256), F...  64.6 us
    unnamed x1, local copies, waits for them, and re-layouts  1.87 us

profile of v2, /device:TPU:1, one launch (start us, length us, event | category | flops | bytes accessed | tf_op | source)
XLA Modules:
  0.0 66.5 jit_solution(11033929731603320620)
XLA Ops:
  0.0 64.6 %shard_map.46 = f32[1,2,256,256]{3,2,1,0:T(8,128)} custom-call(s32[32,32]{1,0:T(8,128)} %ranks.1, f32[1,256,256]{2,1,0:T(8,128)} %diag.1, bf16[1,2,256,128]{3,2,1,0:T(8,128)(2,1)} %left_hbm.1, bf16[1,2,256,128]{3,2,1,0:T(8,128)(2,1)} %right_hbm.1), custom_call_target="tpu_custom_call" | custom-call | tf_op jit(solution)/shard_map/pallas_call | solution.py:421
  64.6 1.9 %copy.6 = f32[1,2,256,256]{3,2,1,0:T(8,128)} copy(f32[1,2,256,256]{3,2,1,0:T(8,128)} %shard_map.46) | data formatting | bytes 1048576

commit v3 on v2

--- a/solution.py
+++ b/solution.py
@@ -81,6 +81,17 @@
                            precision=lax.Precision.HIGHEST, preferred_element_type=F32)
 
 
+def two(v):
+    high = v.astype(jnp.bfloat16)
+    return high, (v - high.astype(F32)).astype(jnp.bfloat16)
+
+
+def nt3(a, b):
+    def one(p, q):
+        return lax.dot_general(p, q, (((1,), (1,)), ((), ())), preferred_element_type=F32)
+    return one(a[0], b[0]) + (one(a[0], b[1]) + one(a[1], b[0]))
+
+
 def front_tile(left, right, rank):
     live = lax.broadcasted_iota(jnp.int32, left.shape, 1) < rank
     left = jnp.where(live, left.astype(F32), 0.0).astype(jnp.bfloat16)
@@ -91,7 +102,7 @@
     def __init__(self, diag, a, bufs, sems):
         self.diag, self.a = diag, a
         (self.d00, self.dd, self.b10, self.col, self.rowb,
-         self.d00p, self.ddp, self.b10p, self.pbuf, self.colz, self.colp) = bufs
+         self.d00p, self.ddp, self.b10p, self.colp) = bufs
         self.ss, self.rs = sems
         self.row = lax.axis_index("row")
         self.c = lax.axis_index("col")
@@ -124,22 +135,39 @@
             pl.when(cond)(lambda: work(lambda copy: copy.start()))
             self.later.append(lambda: pl.when(cond)(lambda: work(lambda copy: copy.wait_send())))
 
+    def greet(self):
+        bar = pltpu.get_barrier_semaphore()
+
+        def tell(**to):
+            pl.semaphore_signal(bar, inc=1, device_id=to, device_id_type=MESH)
+        self.loop(1, 32, lambda d: tell(row=lax.rem(self.row + d, 32)))
+        self.loop(1, 8, lambda d: tell(col=lax.rem(self.z + d, 8) * 2 + self.k))
+        tell(**self.other)
+        for t in range(2):
+            source = self.c + 16 * t
+            for k in range(2):
+                me = jnp.logical_and(source == self.row, self.c == k)
+                pl.when(jnp.logical_and(source >= 2, jnp.logical_not(me)))(
+                    functools.partial(tell, row=source, col=jnp.int32(k)))
+
     def barrier(self):
-        bar = pltpu.get_barrier_semaphore()
-
-        def greet(**to):
-            pl.semaphore_signal(bar, inc=1, device_id=to, device_id_type=MESH)
-        self.loop(1, 32, lambda d: greet(row=lax.rem(self.row + d, 32)))
-        self.loop(1, 8, lambda d: greet(col=lax.rem(self.z + d, 8) * 2 + self.k))
-        greet(**self.other)
-        pl.semaphore_wait(bar, 39)
+        targets = 32 - (lax.rem(self.row, 16) == self.c).astype(jnp.int32)
+        extra = jnp.where(jnp.logical_and(self.z == 0, self.row >= 2), targets, 0)
+        pl.semaphore_wait(pltpu.get_barrier_semaphore(), 39 + extra)
+
+    def from_afar(self, i):
+        def swing(j, half):
+            return half + (j + 1) // 2 * (1 - 2 * lax.rem(j, 2))
+        y = lax.rem(self.y + swing(i // 4, 4), 8)
+        x = lax.rem(self.x + swing(lax.rem(i, 4), 2), 4)
+        return y, x
 
     def scatter(self, cond, src, dst, g):
         def work(act):
-            def one(d):
-                q = lax.rem(self.row + d, 32)
-                act(self.remote(src(8 * lax.rem(q, 4) + q // 4), dst, g, row=q))
-            self.loop(1, 32, one)
+            def one(i):
+                y, x = self.from_afar(i)
+                act(self.remote(src(8 * x + y), dst, g, row=4 * y + x))
+            self.loop(0, 31, one)
         self.run(cond, work)
         pl.when(cond)(lambda: self.local(src(8 * self.x + self.y), dst, g))
 
@@ -207,9 +235,27 @@
     def from_other_core(self, whole, g):
         self.arrived(whole.at[1 - self.k], g + 2)
 
-    def scatter_front(self):
-        a, home = self.a.at[0], self.z == 0
-        self.scatter(home, lambda g: a.at[pl.ds(pl.multiple_of(8 * g, 8), 8), :], self.pbuf.at[self.row], 2)
+    def tile_piece(self, g):
+        return self.a.at[0, pl.ds(pl.multiple_of(8 * g, 8), 8), :]
+
+    def scatter_b10(self):
+        self.scatter(jnp.logical_and(self.row == 1, self.c == 0), self.tile_piece, self.b10p, 5)
+
+    def scatter_cols(self):
+        to, t = lax.rem(self.row, 16), self.row // 16
+        dst = self.colp.at[t, self.k]
+        for s, g in ((0, 2), (1, 8)):
+            sends = jnp.logical_and(jnp.logical_and(self.z == 0, self.row >= 2), t == s)
+
+            def work(act, g=g):
+                def one(i):
+                    y, x = self.from_afar(i)
+                    copy = self.remote(self.tile_piece(8 * x + y), dst, g, row=4 * y + x, col=to)
+                    pl.when(jnp.logical_or(i < 31, to != self.c))(lambda: act(copy))
+                self.loop(0, 32, one)
+            self.run(sends, work)
+            pl.when(jnp.logical_and(sends, to == self.c))(
+                functools.partial(self.local, self.tile_piece(8 * self.x + self.y), dst, g))
 
     def scatter_rows(self):
         a, home = self.a.at[0], self.z == 0
@@ -224,27 +270,11 @@
         self.run(home, along)
         pl.when(home)(lambda: self.local(a, self.rowb.at[self.k], 4))
 
-    def front_to_planes(self):
-        home = self.z == 0
-        pl.when(home)(lambda: self.arrived(self.pbuf, 2))
-
-        def work(act):
-            def one(zz):
-                there = dict(col=2 * zz + self.k)
-
-                @pl.when(self.k == 0)
-                def _():
-                    act(self.remote(self.pbuf.at[1], self.b10p, 5, **there))
-                for t in range(2):
-                    act(self.remote(self.pbuf.at[pl.ds(2 * zz + 16 * t, 2)], self.colz.at[t], 6, **there))
-            self.loop(1, 8, one)
-        self.run(home, work)
-
-        @pl.when(home)
-        def _():
-            for t in range(2):
-                self.local(self.pbuf.at[pl.ds(16 * t, 2)], self.colz.at[t], 6)
-            pl.when(self.k == 0)(lambda: self.local(self.pbuf.at[1], self.b10p, 5))
+    def b10_to_planes(self):
+        home = self.c == 0
+        pl.when(home)(lambda: self.arrived(self.b10p, 5))
+        self.run(home, lambda act: self.loop(1, 8, lambda zz: act(
+            self.remote(self.b10p, self.b10p, 5, col=2 * zz + self.k))))
 
     def rows_along(self):
         away = self.z > 0
@@ -269,18 +299,8 @@
         self.arrived(self.rowb.at[1 - self.k], 7)
 
     def b10_to_other_core(self):
-        pl.when(self.k == 0)(lambda: self.arrived(self.b10p, 5))
+        pl.when(jnp.logical_and(self.k == 0, self.z > 0))(lambda: self.arrived(self.b10p, 5))
         self.run(self.k == 0, lambda act: act(self.remote(self.b10p, self.b10p, 5, **self.other)))
-
-    def cols_to_other_core(self):
-        self.arrived(self.colz, 6)
-
-        def work(act):
-            for t in range(2):
-                act(self.remote(self.colz.at[t, 1 - self.k], self.colp.at[t, self.k], 8, **self.other))
-        self.run(None, work)
-        for t in range(2):
-            self.local(self.colz.at[t, self.k], self.colp.at[t, self.k], 8)
 
     def b10_along_y(self):
         pl.when(self.k == 1)(lambda: self.arrived(self.b10p, 5))
@@ -298,8 +318,9 @@
         return self.needs(4 * y + 3, t)
 
     def cols_along_y(self):
-        self.arrived(self.colp, 8)
         for t in range(2):
+            there = (lambda t=t: self.arrived(self.colp.at[t], (2, 8)[t]))
+            pl.when(self.c >= 2)(there) if t == 0 else there()
             piece, dst, g = self.colp.at[t], self.col.at[t, self.x, self.y], 12 + 2 * t
 
             def work(act, t=t, piece=piece, dst=dst, g=g):
@@ -330,88 +351,129 @@
         a[t] = front_tile(left[0, t], right[0, t], ranks[r, c + 16 * t])
 
 
-def panels(net, out, at):
+def panels(net, out, stages):
     H = 128
     r, c = lax.axis_index("row"), lax.axis_index("col")
     a = net.a
+    done = {}
+
+    def at(name, block=0):
+        for stage in stages.get((name, block), []):
+            stage()
+        for work in works.get((name, block), []):
+            work()
 
     def place(name):
         return lambda block: at(name, block)
-    at("d00", 0)
+
+    def pieces(v):
+        return v[:, :H], v[:, H:]
+
+    def row_first():
+        xa, xb = first(*pieces(net.rowb[0]))
+        done["X"] = [two(xa), two(xb)]
+
+    def row_cross():
+        done["C"] = cross(net.rowb[1], done["X"])
+
+    def row_half():
+        done["Y"] = half(done["C"])
+
+    def first(b0, b1):
+        fa = nt3(two(b0), done["L1"])
+        fb = nt3(two(b1 - nt3(two(fa), done["T1"])), done["L2"])
+        return fa, fb
+
+    def cross(b, X):
+        return b - nt3(X[0], done["Fa"]) - nt3(X[1], done["Fb"])
+
+    def half(C):
+        ya = nt3(two(C[:, :H]), done["L3"])
+        return ya, C[:, H:] - nt3(two(ya), done["T3"])
+
+    works = {("third", 6): [row_first], ("third", 10): [row_cross], ("fourth", 2): [row_half]}
+
+    at("d00")
     A = net.d00[...].reshape(256, H)
     L1 = inverse_factor(A[:H], place("first"))
-    at("a22", 0)
+    at("a22")
     U0 = net.dd[0].reshape(256, H)
     T1 = nt(A[H:], L1)
     L2 = inverse_factor(U0[:H] - nt(T1, T1), place("second"))
-    at("b10", 0)
+    done["L1"], done["T1"], done["L2"] = two(L1), two(T1), two(L2)
+    at("b10")
     B0, B1 = net.b10[0].reshape(256, H), net.b10[1].reshape(256, H)
-
-    def first(B0, B1):
-        Fa = nt(B0, L1)
-        return Fa, nt(B1 - nt(Fa, T1), L2)
-    Fa, Fb = first(B0, B1)
+    Fa = nt(B0, L1)
+    Fb = nt(B1 - nt(Fa, T1), L2)
+    done["Fa"], done["Fb"] = two(Fa), two(Fb)
     U1 = net.dd[1].reshape(256, H)
     L3 = inverse_factor(U0[H:] - nt(Fa[:H], Fa[:H]) - nt(Fb[:H], Fb[:H]), place("third"))
     M21 = U1[:H] - nt(Fa[H:], Fa[:H]) - nt(Fb[H:], Fb[:H])
     T3 = nt(M21, L3)
+    done["L3"], done["T3"] = two(L3), two(T3)
     L4 = inverse_factor(U1[H:] - nt(Fa[H:], Fa[H:]) - nt(Fb[H:], Fb[H:]) - nt(T3, T3), place("fourth"))
-    at("tiles", 0)
-
-    def both(b0, b1):
-        xa, xb = first(b0[:, :H], b0[:, H:])
-        C = b1 - nt(xa, Fa) - nt(xb, Fb)
-        ya = nt(C[:, :H], L3)
-        yb = nt(C[:, H:] - nt(ya, T3), L4)
-        return [jnp.concatenate(p, axis=1) for p in ((xa, xb), (ya, yb))]
-    X, Y = both(net.rowb[0], net.rowb[1])
+    L4 = two(L4)
+    at("tiles")
+    X = done["X"]
+    ya, w = done["Y"]
+    yb = nt3(two(w), L4)
+    rows = X + [two(ya), two(yb)]
     for t in range(2):
         j = c + 16 * t
-        Xj, Yj = both(net.col[t, :, :, 0].reshape(256, 256), net.col[t, :, :, 1].reshape(256, 256))
-        value = a[t] - nt(X, Xj) - nt(Y, Yj)
+        xa, xb = first(*pieces(net.col[t, :, :, 0].reshape(256, 256)))
+        Xj = [two(xa), two(xb)]
+        ja, jw = half(cross(net.col[t, :, :, 1].reshape(256, 256), Xj))
+        jb = nt3(two(jw), L4)
+        value = a[t]
+        for left, right in zip(rows, Xj + [two(ja), two(jb)]):
+            value = value - nt3(left, right)
         if t == 0:
-            value = jnp.where(j == 0, X, jnp.where(j == 1, Y, value))
+            full = [sum(p.astype(F32) for p in v) for v in X] + [ya, yb]
+            value = jnp.where(j == 0, jnp.concatenate(full[:2], axis=1),
+                              jnp.where(j == 1, jnp.concatenate(full[2:], axis=1), value))
         out[0, t] = jnp.where(j < r, value, 0.0)
 
 
 LAND = [(4, 8, 8, 128), (2, 4, 8, 8, 128), (2, 4, 8, 8, 128), (2, 4, 8, 2, 8, 256), (2, 256, 256)]
-PIECES = [(8, 128), (8, 128), (8, 256), (32, 8, 256), (2, 2, 8, 256), (2, 2, 8, 256)]
+PIECES = [(8, 128), (8, 128), (8, 256), (2, 2, 8, 256)]
 
 
 def kernel(ranks, diag, left_hbm, right_hbm, out, left, right, a, *scratch):
-    bufs, (ss, rs, ls) = scratch[:11], scratch[11:]
+    bufs, (ss, rs, ls) = scratch[:9], scratch[9:]
     loads = [pltpu.make_async_copy(left_hbm, left, ls.at[0]), pltpu.make_async_copy(right_hbm, right, ls.at[1])]
     for load in loads:
         load.start()
     t = Traffic(diag, a, bufs, (ss, rs))
-    t.barrier()
-    t.scatter_diag()
+    t.greet()
     for load in loads:
         load.wait()
     own_tiles(ranks, left, right, a)
+    t.barrier()
+    t.scatter_diag()
+    t.scatter_b10()
     t.scatter_rest()
+    t.scatter_cols()
+    t.scatter_rows()
     t.along_y(t.d00p, t.d00, 0, 16)
-    t.scatter_front()
+    t.b10_to_planes()
+    t.along_y(t.ddp, t.dd.at[t.k], 1, 18)
     t.along_x(t.d00, 16)
-    t.scatter_rows()
-    t.along_y(t.ddp, t.dd.at[t.k], 1, 18)
+    t.b10_to_other_core()
+    t.rows_along()
+    t.cols_along_y()
+    t.b10_along_y()
     stages = {
-        ("d00", 0): [lambda: t.all_here(t.d00, 16)],
-        ("first", 6): [lambda: t.along_x(t.dd.at[t.k], 18), t.rows_along],
-        ("first", 11): [t.front_to_planes, lambda: t.to_other_core(t.dd, 18)],
-        ("a22", 0): [lambda: t.from_other_core(t.dd, 18)],
-        ("second", 3): [t.b10_to_other_core, t.cols_to_other_core],
-        ("second", 7): [t.b10_along_y, t.cols_along_y],
-        ("second", 12): [lambda: t.along_x(t.b10.at[t.k], 9)],
-        ("b10", 0): [lambda: t.to_other_core(t.b10, 9), t.cols_along_x, lambda: t.from_other_core(t.b10, 9)],
-        ("third", 8): [t.rows_across],
-        ("tiles", 0): [t.rows_done, t.cols_done],
+        ("d00", 0): [lambda: t.all_here(t.d00, 16), lambda: t.along_x(t.dd.at[t.k], 18)],
+        ("first", 12): [lambda: t.to_other_core(t.dd, 18)],
+        ("a22", 0): [lambda: t.along_x(t.b10.at[t.k], 9), lambda: t.from_other_core(t.dd, 18)],
+        ("second", 5): [t.cols_along_x],
+        ("second", 12): [lambda: t.to_other_core(t.b10, 9)],
+        ("b10", 0): [lambda: t.from_other_core(t.b10, 9)],
+        ("third", 1): [t.rows_across],
+        ("third", 6): [t.rows_done],
+        ("tiles", 0): [t.cols_done],
     }
-
-    def at(name, block):
-        for stage in stages.get((name, block), []):
-            stage()
-    panels(t, out, at)
+    panels(t, out, stages)
     t.finish()
 
 

time: 66.8 us -> 57.6 us (0.86)
  Pallas kernels: 64.6 us -> 55.5 us
    pallas_call x1, Pallas kernels: 64.6 us -> 55.5 us  [shards(): pl.pallas_call(kernel, out_shape=jax.ShapeDtypeStruct((1, 2, 256, 256), F...]
where the time goes in v3:
time: 57.6 us; the launch traced here: 57.4 us
  Pallas kernels  55.5 us (96%)
  local copies, waits for them, and re-layouts  1.87 us (3%)
    pallas_call x1, Pallas kernels, shards(): pl.pallas_call(kernel, out_shape=jax.ShapeDtypeStruct((1, 2, 256, 256), F...  55.5 us
    unnamed x1, local copies, waits for them, and re-layouts  1.87 us

profile of v3, /device:TPU:1, one launch (start us, length us, event | category | flops | bytes accessed | tf_op | source)
XLA Modules:
  0.0 57.4 jit_solution(10896821285094191343)
XLA Ops:
  0.0 55.5 %shard_map.46 = f32[1,2,256,256]{3,2,1,0:T(8,128)} custom-call(s32[32,32]{1,0:T(8,128)} %ranks.1, f32[1,256,256]{2,1,0:T(8,128)} %diag.1, bf16[1,2,256,128]{3,2,1,0:T(8,128)(2,1)} %left_hbm.1, bf16[1,2,256,128]{3,2,1,0:T(8,128)(2,1)} %right_hbm.1), custom_call_target="tpu_custom_call" | custom-call | tf_op jit(solution)/shard_map/pallas_call | solution.py:483
  55.5 1.9 %copy.6 = f32[1,2,256,256]{3,2,1,0:T(8,128)} copy(f32[1,2,256,256]{3,2,1,0:T(8,128)} %shard_map.46) | data formatting | bytes 1048576

commit v4 on v3

--- a/solution.py
+++ b/solution.py
@@ -102,7 +102,7 @@
     def __init__(self, diag, a, bufs, sems):
         self.diag, self.a = diag, a
         (self.d00, self.dd, self.b10, self.col, self.rowb,
-         self.d00p, self.ddp, self.b10p, self.colp) = bufs
+         self.d00p, self.ddp, self.b10z, self.b10p, self.colp) = bufs
         self.ss, self.rs = sems
         self.row = lax.axis_index("row")
         self.c = lax.axis_index("col")
@@ -127,22 +127,33 @@
             return carry
         lax.fori_loop(lo, hi, step, 0)
 
-    def run(self, cond, work):
+    def run(self, cond, work, g, rows, lanes=128, times=None):
+        ref = self.rowb.at[0, pl.ds(0, rows), pl.ds(0, lanes)]
+
+        def wait():
+            def one(_=0):
+                pltpu.make_async_copy(ref, ref, self.ss.at[g]).wait()
+            one() if times is None else self.loop(0, times, one)
+
         if cond is None:
             work(lambda copy: copy.start())
-            self.later.append(lambda: work(lambda copy: copy.wait_send()))
+            self.later.append(wait)
         else:
             pl.when(cond)(lambda: work(lambda copy: copy.start()))
-            self.later.append(lambda: pl.when(cond)(lambda: work(lambda copy: copy.wait_send())))
+            self.later.append(lambda: pl.when(cond)(wait))
 
     def greet(self):
         bar = pltpu.get_barrier_semaphore()
 
         def tell(**to):
             pl.semaphore_signal(bar, inc=1, device_id=to, device_id_type=MESH)
-        self.loop(1, 32, lambda d: tell(row=lax.rem(self.row + d, 32)))
+        self.loop(1, 8, lambda d: tell(row=4 * lax.rem(self.y + d, 8) + self.x))
+        self.loop(1, 4, lambda d: tell(row=4 * self.y + lax.rem(self.x + d, 4)))
         self.loop(1, 8, lambda d: tell(col=lax.rem(self.z + d, 8) * 2 + self.k))
         tell(**self.other)
+        pl.when(self.k == 1)(lambda: tell(col=jnp.int32(0)))
+        for root in range(2):
+            pl.when(self.row != root)(functools.partial(tell, row=jnp.int32(root)))
         for t in range(2):
             source = self.c + 16 * t
             for k in range(2):
@@ -153,7 +164,8 @@
     def barrier(self):
         targets = 32 - (lax.rem(self.row, 16) == self.c).astype(jnp.int32)
         extra = jnp.where(jnp.logical_and(self.z == 0, self.row >= 2), targets, 0)
-        pl.semaphore_wait(pltpu.get_barrier_semaphore(), 39 + extra)
+        extra = extra + jnp.where(self.row < 2, 31, 0) + jnp.where(self.c == 0, 8, 0)
+        pl.semaphore_wait(pltpu.get_barrier_semaphore(), 18 + extra)
 
     def from_afar(self, i):
         def swing(j, half):
@@ -162,20 +174,20 @@
         x = lax.rem(self.x + swing(lax.rem(i, 4), 2), 4)
         return y, x
 
-    def scatter(self, cond, src, dst, g):
+    def scatter(self, cond, src, dst, g, lanes):
         def work(act):
             def one(i):
                 y, x = self.from_afar(i)
                 act(self.remote(src(8 * x + y), dst, g, row=4 * y + x))
             self.loop(0, 31, one)
-        self.run(cond, work)
+        self.run(cond, work, g, 248, lanes)
         pl.when(cond)(lambda: self.local(src(8 * self.x + self.y), dst, g))
 
     def block(self, rows, half):
         return self.diag.at[0, pl.ds(pl.multiple_of(rows, 8), 8), pl.ds(128 * half, 128)]
 
     def scatter_diag(self):
-        self.scatter(self.row == 0, lambda g: self.block(8 * g, 0), self.d00p, 0)
+        self.scatter(self.row == 0, lambda g: self.block(8 * g, 0), self.d00p, 0, 128)
 
     def scatter_rest(self):
         for root, k, lo, rows, half in ((0, 0, 0, 128, 1), (1, 0, 16, 0, 0), (1, 1, 0, 128, 0), (1, 1, 16, 128, 1)):
@@ -188,49 +200,37 @@
                     src = self.block(rows + 8 * i, half)
                     pl.when(q != root)(lambda: act(self.remote(src, self.ddp, 1, row=q)))
                 self.loop(0, 16, one)
-            self.run(mine, work)
             own = 8 * root - lo
+            self.run(mine, work, 1, 120 if 0 <= own < 16 else 128)
             if 0 <= own < 16:
                 pl.when(mine)(lambda: self.local(self.block(rows + 8 * own, half), self.ddp, 1))
 
-    def along_y(self, piece, whole, pg, g, pred=None):
+    def along_y(self, piece, whole, pg, g):
         self.arrived(piece, pg)
         dst = whole.at[self.x, self.y]
 
         def work(act):
             def one(d):
-                y = lax.rem(self.y + d, 8)
-                copy = self.remote(piece, dst, g, row=4 * y + self.x)
-                if pred is None:
-                    act(copy)
-                else:
-                    pl.when(pred(y))(lambda: act(copy))
+                act(self.remote(piece, dst, g, row=4 * lax.rem(self.y + d, 8) + self.x))
             self.loop(1, 8, one)
-        self.run(None, work)
-        mine = lambda: self.local(piece, dst, g)
-        mine() if pred is None else pl.when(pred(self.y))(mine)
-
-    def along_x(self, whole, g, pred=None, line=None):
+        self.run(None, work, g, 56)
+        self.local(piece, dst, g)
+
+    def along_x(self, whole, g):
         held = whole.at[self.x]
-        here = lambda: self.arrived(held, g)
-        here() if line is None else pl.when(line(self.y))(here)
+        self.arrived(held, g)
 
         def work(act):
-            for d in (1, 3, 2):
-                x = lax.rem(self.x + d, 4)
-                copy = self.remote(held, held, g + 1, row=4 * self.y + x)
-                if pred is None:
-                    act(copy)
-                else:
-                    pl.when(pred(4 * self.y + x))(functools.partial(act, copy))
-        self.run(None, work)
+            for d in (2, 1, 3):
+                act(self.remote(held, held, g + 1, row=4 * self.y + lax.rem(self.x + d, 4)))
+        self.run(None, work, g + 1, 192)
 
     def all_here(self, whole, g):
         self.arrived(whole.at[pl.ds(0, 3)], g + 1)
 
     def to_other_core(self, whole, g):
         self.all_here(whole.at[self.k], g)
-        self.run(None, lambda act: act(self.remote(whole.at[self.k], whole.at[self.k], g + 2, **self.other)))
+        self.run(None, lambda act: act(self.remote(whole.at[self.k], whole.at[self.k], g + 2, **self.other)), g + 2, 256)
 
     def from_other_core(self, whole, g):
         self.arrived(whole.at[1 - self.k], g + 2)
@@ -239,7 +239,7 @@
         return self.a.at[0, pl.ds(pl.multiple_of(8 * g, 8), 8), :]
 
     def scatter_b10(self):
-        self.scatter(jnp.logical_and(self.row == 1, self.c == 0), self.tile_piece, self.b10p, 5)
+        self.scatter(jnp.logical_and(self.row == 1, self.c == 0), self.tile_piece, self.b10z, 5, 256)
 
     def scatter_cols(self):
         to, t = lax.rem(self.row, 16), self.row // 16
@@ -253,7 +253,9 @@
                     copy = self.remote(self.tile_piece(8 * x + y), dst, g, row=4 * y + x, col=to)
                     pl.when(jnp.logical_or(i < 31, to != self.c))(lambda: act(copy))
                 self.loop(0, 32, one)
-            self.run(sends, work)
+            here = to == self.c
+            self.run(jnp.logical_and(sends, jnp.logical_not(here)), work, g, 256, 256)
+            self.run(jnp.logical_and(sends, here), work, g, 248, 256)
             pl.when(jnp.logical_and(sends, to == self.c))(
                 functools.partial(self.local, self.tile_piece(8 * self.x + self.y), dst, g))
 
@@ -265,16 +267,21 @@
                 there = dict(col=2 * zz + self.k)
                 rows = pl.ds(pl.multiple_of(32 * zz, 32), 32)
                 act(self.remote(a.at[rows, :], self.rowb.at[self.k, rows, :], 3, **there))
-                act(self.remote(a.at[pl.ds(0, 32), :], self.rowb.at[self.k, pl.ds(0, 32), :], 4, **there))
             self.loop(1, 8, one)
-        self.run(home, along)
+        self.run(home, along, 3, 224, 256)
         pl.when(home)(lambda: self.local(a, self.rowb.at[self.k], 4))
 
     def b10_to_planes(self):
         home = self.c == 0
-        pl.when(home)(lambda: self.arrived(self.b10p, 5))
-        self.run(home, lambda act: self.loop(1, 8, lambda zz: act(
-            self.remote(self.b10p, self.b10p, 5, col=2 * zz + self.k))))
+        pl.when(home)(lambda: self.arrived(self.b10z, 5))
+
+        def work(act):
+            def one(c):
+                half = self.b10z.at[:, pl.ds(pl.multiple_of(128 * lax.rem(c, 2), 128), 128)]
+                act(self.remote(half, self.b10p, 6, col=c))
+            self.loop(1, 16, one)
+        self.run(home, work, 6, 120)
+        pl.when(home)(lambda: self.local(self.b10z.at[:, pl.ds(0, 128)], self.b10p, 6))
 
     def rows_along(self):
         away = self.z > 0
@@ -287,28 +294,19 @@
                 zz = 1 + lax.rem(self.z - 1 + d, 7)
                 act(self.remote(held.at[mine, :], held.at[mine, :], 4, col=2 * zz + self.k))
             self.loop(1, 7, one)
-        self.run(away, work)
+        self.run(away, work, 4, 192, 256)
+        first = self.a.at[0, pl.ds(0, 32), :]
+        self.run(self.z == 0, lambda act: self.loop(1, 8, lambda zz: act(
+            self.remote(first, held.at[pl.ds(0, 32), :], 4, col=2 * zz + self.k))), 4, 224, 256)
 
     def rows_across(self):
         held = self.rowb.at[self.k]
         pl.when(self.z > 0)(lambda: self.arrived(held.at[pl.ds(0, 224), :], 4))
         pl.when(self.z == 0)(lambda: self.arrived(held, 4))
-        self.run(None, lambda act: act(self.remote(held, held, 7, **self.other)))
+        self.run(None, lambda act: act(self.remote(held, held, 7, **self.other)), 7, 256, 256)
 
     def rows_done(self):
         self.arrived(self.rowb.at[1 - self.k], 7)
-
-    def b10_to_other_core(self):
-        pl.when(jnp.logical_and(self.k == 0, self.z > 0))(lambda: self.arrived(self.b10p, 5))
-        self.run(self.k == 0, lambda act: act(self.remote(self.b10p, self.b10p, 5, **self.other)))
-
-    def b10_along_y(self):
-        pl.when(self.k == 1)(lambda: self.arrived(self.b10p, 5))
-        half = self.b10p.at[:, pl.ds(pl.multiple_of(128 * self.k, 128), 128)]
-        dst = self.b10.at[self.k, self.x, self.y]
-        self.run(None, lambda act: self.loop(1, 8, lambda d: act(
-            self.remote(half, dst, 9, row=4 * lax.rem(self.y + d, 8) + self.x))))
-        self.local(half, dst, 9)
 
     def needs(self, q, t):
         below = q > self.c + 16 * t
@@ -328,13 +326,20 @@
                     y = lax.rem(self.y + d, 8)
                     pl.when(self.line_needs(y, t))(lambda: act(self.remote(piece, dst, g, row=4 * y + self.x)))
                 self.loop(1, 8, one)
-            self.run(None, work)
+            lines = sum(self.line_needs(lax.rem(self.y + d, 8), t).astype(jnp.int32) for d in range(1, 8))
+            self.run(None, work, g, 16, 256, lines)
             pl.when(self.line_needs(self.y, t))(functools.partial(self.local, piece, dst, g))
 
     def cols_along_x(self):
         for t in range(2):
-            self.along_x(self.col.at[t], 12 + 2 * t, functools.partial(self.needs, t=t),
-                         functools.partial(self.line_needs, t=t))
+            held, g = self.col.at[t, self.x], 13 + 2 * t
+            pl.when(self.line_needs(self.y, t))(functools.partial(self.arrived, held, g - 1))
+            others = [4 * self.y + lax.rem(self.x + d, 4) for d in (2, 1, 3)]
+
+            def work(act, t=t, held=held, g=g, others=others):
+                for q in others:
+                    pl.when(self.needs(q, t))(lambda: act(self.remote(held, held, g, row=q)))
+            self.run(None, work, g, 128, 256, sum(self.needs(q, t).astype(jnp.int32) for q in others))
 
     def cols_done(self):
         for t in range(2):
@@ -366,12 +371,8 @@
     def place(name):
         return lambda block: at(name, block)
 
-    def pieces(v):
-        return v[:, :H], v[:, H:]
-
     def row_first():
-        xa, xb = first(*pieces(net.rowb[0]))
-        done["X"] = [two(xa), two(xb)]
+        done["X"] = two(first(net.rowb[0]))
 
     def row_cross():
         done["C"] = cross(net.rowb[1], done["X"])
@@ -379,19 +380,17 @@
     def row_half():
         done["Y"] = half(done["C"])
 
-    def first(b0, b1):
-        fa = nt3(two(b0), done["L1"])
-        fb = nt3(two(b1 - nt3(two(fa), done["T1"])), done["L2"])
-        return fa, fb
+    def first(b):
+        return nt3(two(b), done["inverse"])
 
     def cross(b, X):
-        return b - nt3(X[0], done["Fa"]) - nt3(X[1], done["Fb"])
+        return b - nt3(X, done["F"])
 
     def half(C):
         ya = nt3(two(C[:, :H]), done["L3"])
         return ya, C[:, H:] - nt3(two(ya), done["T3"])
 
-    works = {("third", 6): [row_first], ("third", 10): [row_cross], ("fourth", 2): [row_half]}
+    works = {("third", 5): [row_first], ("third", 9): [row_cross], ("fourth", 2): [row_half]}
 
     at("d00")
     A = net.d00[...].reshape(256, H)
@@ -400,46 +399,46 @@
     U0 = net.dd[0].reshape(256, H)
     T1 = nt(A[H:], L1)
     L2 = inverse_factor(U0[:H] - nt(T1, T1), place("second"))
-    done["L1"], done["T1"], done["L2"] = two(L1), two(T1), two(L2)
+    X1 = lax.dot(T1, L1, precision=lax.Precision.HIGHEST)
+    X1 = lax.dot(L2, X1, precision=lax.Precision.HIGHEST)
+    inverse = jnp.concatenate([jnp.concatenate([L1, jnp.zeros_like(L1)], axis=1),
+                               jnp.concatenate([-X1, L2], axis=1)], axis=0)
+    done["inverse"] = two(inverse)
     at("b10")
-    B0, B1 = net.b10[0].reshape(256, H), net.b10[1].reshape(256, H)
-    Fa = nt(B0, L1)
-    Fb = nt(B1 - nt(Fa, T1), L2)
-    done["Fa"], done["Fb"] = two(Fa), two(Fb)
+    F = nt(jnp.concatenate([net.b10[0].reshape(256, H), net.b10[1].reshape(256, H)], axis=1), inverse)
+    done["F"] = two(F)
     U1 = net.dd[1].reshape(256, H)
-    L3 = inverse_factor(U0[H:] - nt(Fa[:H], Fa[:H]) - nt(Fb[:H], Fb[:H]), place("third"))
-    M21 = U1[:H] - nt(Fa[H:], Fa[:H]) - nt(Fb[H:], Fb[:H])
+    L3 = inverse_factor(U0[H:] - nt(F[:H], F[:H]), place("third"))
+    M21 = U1[:H] - nt(F[H:], F[:H])
     T3 = nt(M21, L3)
     done["L3"], done["T3"] = two(L3), two(T3)
-    L4 = inverse_factor(U1[H:] - nt(Fa[H:], Fa[H:]) - nt(Fb[H:], Fb[H:]) - nt(T3, T3), place("fourth"))
+    L4 = inverse_factor(U1[H:] - nt(F[H:], F[H:]) - nt(T3, T3), place("fourth"))
     L4 = two(L4)
     at("tiles")
     X = done["X"]
     ya, w = done["Y"]
     yb = nt3(two(w), L4)
-    rows = X + [two(ya), two(yb)]
+    rows = [X, two(ya), two(yb)]
     for t in range(2):
         j = c + 16 * t
-        xa, xb = first(*pieces(net.col[t, :, :, 0].reshape(256, 256)))
-        Xj = [two(xa), two(xb)]
+        Xj = two(first(net.col[t, :, :, 0].reshape(256, 256)))
         ja, jw = half(cross(net.col[t, :, :, 1].reshape(256, 256), Xj))
         jb = nt3(two(jw), L4)
         value = a[t]
-        for left, right in zip(rows, Xj + [two(ja), two(jb)]):
+        for left, right in zip(rows, [Xj, two(ja), two(jb)]):
             value = value - nt3(left, right)
         if t == 0:
-            full = [sum(p.astype(F32) for p in v) for v in X] + [ya, yb]
-            value = jnp.where(j == 0, jnp.concatenate(full[:2], axis=1),
-                              jnp.where(j == 1, jnp.concatenate(full[2:], axis=1), value))
+            value = jnp.where(j == 0, X[0].astype(F32) + X[1].astype(F32),
+                              jnp.where(j == 1, jnp.concatenate([ya, yb], axis=1), value))
         out[0, t] = jnp.where(j < r, value, 0.0)
 
 
 LAND = [(4, 8, 8, 128), (2, 4, 8, 8, 128), (2, 4, 8, 8, 128), (2, 4, 8, 2, 8, 256), (2, 256, 256)]
-PIECES = [(8, 128), (8, 128), (8, 256), (2, 2, 8, 256)]
+PIECES = [(8, 128), (8, 128), (8, 256), (8, 128), (2, 2, 8, 256)]
 
 
 def kernel(ranks, diag, left_hbm, right_hbm, out, left, right, a, *scratch):
-    bufs, (ss, rs, ls) = scratch[:9], scratch[9:]
+    bufs, (ss, rs, ls) = scratch[:10], scratch[10:]
     loads = [pltpu.make_async_copy(left_hbm, left, ls.at[0]), pltpu.make_async_copy(right_hbm, right, ls.at[1])]
     for load in loads:
         load.start()
@@ -449,28 +448,25 @@
         load.wait()
     own_tiles(ranks, left, right, a)
     t.barrier()
+    t.scatter_b10()
     t.scatter_diag()
-    t.scatter_b10()
     t.scatter_rest()
+    t.scatter_rows()
     t.scatter_cols()
-    t.scatter_rows()
     t.along_y(t.d00p, t.d00, 0, 16)
     t.b10_to_planes()
     t.along_y(t.ddp, t.dd.at[t.k], 1, 18)
+    t.rows_along()
     t.along_x(t.d00, 16)
-    t.b10_to_other_core()
-    t.rows_along()
+    t.along_y(t.b10p, t.b10.at[t.k], 6, 9)
+    t.along_x(t.dd.at[t.k], 18)
     t.cols_along_y()
-    t.b10_along_y()
     stages = {
-        ("d00", 0): [lambda: t.all_here(t.d00, 16), lambda: t.along_x(t.dd.at[t.k], 18)],
-        ("first", 12): [lambda: t.to_other_core(t.dd, 18)],
-        ("a22", 0): [lambda: t.along_x(t.b10.at[t.k], 9), lambda: t.from_other_core(t.dd, 18)],
-        ("second", 5): [t.cols_along_x],
-        ("second", 12): [lambda: t.to_other_core(t.b10, 9)],
-        ("b10", 0): [lambda: t.from_other_core(t.b10, 9)],
+        ("d00", 0): [lambda: t.all_here(t.d00, 16)],
+        ("a22", 0): [lambda: t.to_other_core(t.dd, 18), lambda: t.along_x(t.b10.at[t.k], 9), lambda: t.from_other_core(t.dd, 18)],
+        ("b10", 0): [lambda: t.to_other_core(t.b10, 9), t.cols_along_x, lambda: t.from_other_core(t.b10, 9)],
         ("third", 1): [t.rows_across],
-        ("third", 6): [t.rows_done],
+        ("third", 4): [t.rows_done],
         ("tiles", 0): [t.cols_done],
     }
     panels(t, out, stages)

time: 57.6 us -> 55 us (0.955)
  Pallas kernels: 55.5 us -> 52.8 us
    pallas_call x1, Pallas kernels: 55.5 us -> 52.8 us  [shards(): pl.pallas_call(kernel, out_shape=jax.ShapeDtypeStruct((1, 2, 256, 256), F...]
where the time goes in v4:
time: 55 us; the launch traced here: 54.7 us
  Pallas kernels  52.8 us (96%)
  local copies, waits for them, and re-layouts  1.87 us (3%)
    pallas_call x1, Pallas kernels, shards(): pl.pallas_call(kernel, out_shape=jax.ShapeDtypeStruct((1, 2, 256, 256), F...  52.8 us
    unnamed x1, local copies, waits for them, and re-layouts  1.87 us

profile of v4, /device:TPU:1, one launch (start us, length us, event | category | flops | bytes accessed | tf_op | source)
XLA Modules:
  0.0 54.7 jit_solution(11513846378031074557)
XLA Ops:
  0.0 52.8 %shard_map.46 = f32[1,2,256,256]{3,2,1,0:T(8,128)} custom-call(s32[32,32]{1,0:T(8,128)} %ranks.1, f32[1,256,256]{2,1,0:T(8,128)} %diag.1, bf16[1,2,256,128]{3,2,1,0:T(8,128)(2,1)} %left_hbm.1, bf16[1,2,256,128]{3,2,1,0:T(8,128)(2,1)} %right_hbm.1), custom_call_target="tpu_custom_call" | custom-call | tf_op jit(solution)/shard_map/pallas_call | solution.py:479
  52.8 1.9 %copy.6 = f32[1,2,256,256]{3,2,1,0:T(8,128)} copy(f32[1,2,256,256]{3,2,1,0:T(8,128)} %shard_map.46) | data formatting | bytes 1048576

commit v5 on v4

--- a/solution.py
+++ b/solution.py
@@ -76,9 +76,19 @@
     return jnp.concatenate(out, axis=0)
 
 
+def parts(v):
+    high = v.astype(jnp.bfloat16)
+    rest = v - high.astype(F32)
+    middle = rest.astype(jnp.bfloat16)
+    return high, middle, (rest - middle.astype(F32)).astype(jnp.bfloat16)
+
+
 def nt(a, b):
-    return lax.dot_general(a, b, (((1,), (1,)), ((), ())),
-                           precision=lax.Precision.HIGHEST, preferred_element_type=F32)
+    a1, a2, a3 = parts(a)
+    b1, b2, b3 = parts(b)
+    return lax.dot_general(jnp.concatenate([a3, a2, a1, a2, a1, a1], axis=1),
+                           jnp.concatenate([b1, b2, b3, b1, b2, b1], axis=1),
+                           (((1,), (1,)), ((), ())), preferred_element_type=F32)
 
 
 def two(v):
@@ -377,6 +387,13 @@
     def row_cross():
         done["C"] = cross(net.rowb[1], done["X"])
 
+    def col_first(t):
+        done["col", t] = two(first(net.col[t, :, :, 0].reshape(256, 256)))
+
+    def col_half(t):
+        Xj = done["col", t]
+        done["tile", t] = Xj, half(cross(net.col[t, :, :, 1].reshape(256, 256), Xj))
+
     def row_half():
         done["Y"] = half(done["C"])
 
@@ -390,7 +407,9 @@
         ya = nt3(two(C[:, :H]), done["L3"])
         return ya, C[:, H:] - nt3(two(ya), done["T3"])
 
-    works = {("third", 5): [row_first], ("third", 9): [row_cross], ("fourth", 2): [row_half]}
+    works = {("third", 5): [row_first], ("third", 9): [row_cross], ("fourth", 2): [row_half],
+             ("fourth", 10): [functools.partial(col_first, 0)], ("fourth", 11): [functools.partial(col_first, 1)],
+             ("fourth", 12): [functools.partial(col_half, 0)], ("fourth", 14): [functools.partial(col_half, 1)]}
 
     at("d00")
     A = net.d00[...].reshape(256, H)
@@ -421,8 +440,7 @@
     rows = [X, two(ya), two(yb)]
     for t in range(2):
         j = c + 16 * t
-        Xj = two(first(net.col[t, :, :, 0].reshape(256, 256)))
-        ja, jw = half(cross(net.col[t, :, :, 1].reshape(256, 256), Xj))
+        Xj, (ja, jw) = done["tile", t]
         jb = nt3(two(jw), L4)
         value = a[t]
         for left, right in zip(rows, [Xj, two(ja), two(jb)]):
@@ -467,7 +485,7 @@
         ("b10", 0): [lambda: t.to_other_core(t.b10, 9), t.cols_along_x, lambda: t.from_other_core(t.b10, 9)],
         ("third", 1): [t.rows_across],
         ("third", 4): [t.rows_done],
-        ("tiles", 0): [t.cols_done],
+        ("fourth", 9): [t.cols_done],
     }
     panels(t, out, stages)
     t.finish()

time: 55 us -> 53 us (0.964)
  Pallas kernels: 52.8 us -> 50.8 us
    pallas_call x1, Pallas kernels: 52.8 us -> 50.8 us  [shards(): pl.pallas_call(kernel, out_shape=jax.ShapeDtypeStruct((1, 2, 256, 256), F...]
where the time goes in v5:
time: 53 us; the launch traced here: 52.7 us
  Pallas kernels  50.8 us (96%)
  local copies, waits for them, and re-layouts  1.87 us (4%)
    pallas_call x1, Pallas kernels, shards(): pl.pallas_call(kernel, out_shape=jax.ShapeDtypeStruct((1, 2, 256, 256), F...  50.8 us
    unnamed x1, local copies, waits for them, and re-layouts  1.87 us

profile of v5, /device:TPU:1, one launch (start us, length us, event | category | flops | bytes accessed | tf_op | source)
XLA Modules:
  0.0 52.7 jit_solution(16649802571197428743)
XLA Ops:
  0.0 50.8 %shard_map.46 = f32[1,2,256,256]{3,2,1,0:T(8,128)} custom-call(s32[32,32]{1,0:T(8,128)} %ranks.1, f32[1,256,256]{2,1,0:T(8,128)} %diag.1, bf16[1,2,256,128]{3,2,1,0:T(8,128)(2,1)} %left_hbm.1, bf16[1,2,256,128]{3,2,1,0:T(8,128)(2,1)} %right_hbm.1), custom_call_target="tpu_custom_call" | custom-call | tf_op jit(solution)/shard_map/pallas_call | solution.py:497
  50.8 1.9 %copy.6 = f32[1,2,256,256]{3,2,1,0:T(8,128)} copy(f32[1,2,256,256]{3,2,1,0:T(8,128)} %shard_map.46) | data formatting | bytes 1048576

commit v6 on v5

--- a/solution.py
+++ b/solution.py
@@ -65,13 +65,20 @@
         if not last:
             z = [down(rk, k) for k in range(8)]
             ze = [down(ek, k) for k in range(8)]
-            for I in range(K + 1, n):
+            for I in range(K + 1, min(K + 5, n)):
                 c = below_old if I == K + 1 else [across(R[I], 8 * K + j) for j in range(8)]
-                a, b = R[I], E[I]
                 for k in range(8):
-                    a = a - c[k] * z[k]
-                    b = b - c[k] * ze[k]
-                R[I], E[I] = a, b
+                    R[I] = R[I] - c[k] * z[k]
+                    E[I] = E[I] - c[k] * ze[k]
+            if K + 5 < n:
+                a1, a2, a3 = [v.astype(F32) for v in parts(R[K])]
+                b1, b2, b3 = [v.astype(F32) for v in parts(jnp.concatenate([rk, ek], axis=1))]
+                less = lax.dot_general(jnp.concatenate([a1, a1, a2, a1, a3, a2], axis=0).astype(jnp.bfloat16),
+                                       jnp.concatenate([b1, b2, b1, b3, b1, b2], axis=0).astype(jnp.bfloat16),
+                                       (((0,), (0,)), ((), ())), preferred_element_type=F32)
+                for I in range(K + 5, n):
+                    R[I] = R[I] - less[8 * I:8 * I + 8, :128]
+                    E[I] = E[I] - less[8 * I:8 * I + 8, 128:]
             here = after
     return jnp.concatenate(out, axis=0)
 
@@ -455,9 +462,10 @@
 PIECES = [(8, 128), (8, 128), (8, 256), (8, 128), (2, 2, 8, 256)]
 
 
-def kernel(ranks, diag, left_hbm, right_hbm, out, left, right, a, *scratch):
+def kernel(ranks, diag_hbm, left_hbm, right_hbm, out, left, right, a, diag, *scratch):
     bufs, (ss, rs, ls) = scratch[:10], scratch[10:]
-    loads = [pltpu.make_async_copy(left_hbm, left, ls.at[0]), pltpu.make_async_copy(right_hbm, right, ls.at[1])]
+    loads = [pltpu.make_async_copy(left_hbm, left, ls.at[0]), pltpu.make_async_copy(right_hbm, right, ls.at[1]),
+             pltpu.make_async_copy(diag_hbm, diag, ls.at[2])]
     for load in loads:
         load.start()
     t = Traffic(diag, a, bufs, (ss, rs))
@@ -482,8 +490,10 @@
     stages = {
         ("d00", 0): [lambda: t.all_here(t.d00, 16)],
         ("a22", 0): [lambda: t.to_other_core(t.dd, 18), lambda: t.along_x(t.b10.at[t.k], 9), lambda: t.from_other_core(t.dd, 18)],
-        ("b10", 0): [lambda: t.to_other_core(t.b10, 9), t.cols_along_x, lambda: t.from_other_core(t.b10, 9)],
-        ("third", 1): [t.rows_across],
+        ("second", 14): [lambda: t.to_other_core(t.b10, 9)],
+        ("b10", 0): [lambda: t.from_other_core(t.b10, 9)],
+        ("third", 0): [t.cols_along_x],
+        ("third", 2): [t.rows_across],
         ("third", 4): [t.rows_done],
         ("fourth", 9): [t.cols_done],
     }
@@ -499,9 +509,9 @@
         out_shape=jax.ShapeDtypeStruct((1, 2, 256, 256), F32),
         in_specs=[pl.BlockSpec(memory_space=pltpu.SMEM), hbm, hbm, hbm],
         out_specs=pl.BlockSpec(memory_space=pltpu.VMEM),
-        scratch_shapes=[V((1, 2, 256, 128), jnp.bfloat16), V((1, 2, 256, 128), jnp.bfloat16), V((2, 256, 256), F32)]
+        scratch_shapes=[V((1, 2, 256, 128), jnp.bfloat16), V((1, 2, 256, 128), jnp.bfloat16), V((2, 256, 256), F32), V((1, 256, 256), F32)]
         + [V(s, F32) for s in LAND + PIECES]
-        + [pltpu.SemaphoreType.DMA((21,)), pltpu.SemaphoreType.DMA((21,)), pltpu.SemaphoreType.DMA((2,))],
+        + [pltpu.SemaphoreType.DMA((21,)), pltpu.SemaphoreType.DMA((21,)), pltpu.SemaphoreType.DMA((3,))],
         compiler_params=pltpu.CompilerParams(collective_id=0, has_side_effects=True, vmem_limit_bytes=60 << 20),
     )(ranks, diag, left, right)
 

time: 53 us -> 52.7 us (level)
  no operation moved by 1% of the time
where the time goes in v6:
time: 52.7 us; the launch traced here: 52.3 us
  Pallas kernels  50.4 us (96%)
  local copies, waits for them, and re-layouts  1.87 us (4%)
    pallas_call x1, Pallas kernels, shards(): pl.pallas_call(kernel, out_shape=jax.ShapeDtypeStruct((1, 2, 256, 256), F...  50.4 us
    unnamed x1, local copies, waits for them, and re-layouts  1.87 us

profile of v6, /device:TPU:1, one launch (start us, length us, event | category | flops | bytes accessed | tf_op | source)
XLA Modules:
  0.0 52.3 jit_solution(7700188112011158689)
XLA Ops:
  0.0 50.4 %shard_map.46 = f32[1,2,256,256]{3,2,1,0:T(8,128)} custom-call(s32[32,32]{1,0:T(8,128)} %ranks.1, f32[1,256,256]{2,1,0:T(8,128)} %diag_hbm.1, bf16[1,2,256,128]{3,2,1,0:T(8,128)(2,1)} %left_hbm.1, bf16[1,2,256,128]{3,2,1,0:T(8,128)(2,1)} %right_hbm.1), custom_call_target="tpu_custom_call" | custom-call | tf_op jit(solution)/shard_map/pallas_call | solution.py:507
  50.5 1.9 %copy.6 = f32[1,2,256,256]{3,2,1,0:T(8,128)} copy(f32[1,2,256,256]{3,2,1,0:T(8,128)} %shard_map.46) | data formatting | bytes 1048576
